TPU v7x, 256 devices: a whole 4x4x8 slice. The times are simulated.
256 devices in a mesh: nodes: 64 (over x, z, core), feat: 4 (over y).
Axes of the slice: x: 4, y: 4, z: 8, core: 2. Of those that a mesh axis runs over, the one named last changes fastest.
Arguments:
- x_t: bfloat16 [128, 131072], P('feat', 'nodes'), may hold values from -6 to 6
- weight: bfloat16 [128, 256], P(None, 'feat'), may hold values from -0.5 to 0.5
- cotangent: bfloat16 [256, 131072], P('feat', 'nodes'), may hold values from -6 to 6
- self_tiles: bfloat16 [1024, 128, 128], P('nodes'), may hold values from -0.125 to 0.125
- hub_tiles: bfloat16 [1024, 8, 128, 128], P('nodes'), may hold values from -0.125 to 0.125
- nbr_tiles: bfloat16 [1024, 8, 128, 128], P('nodes'), may hold values from -0.125 to 0.125
- hub_ids: int32 [8], replicated, may hold values from 0 to 1023
- send_list: int32 [64, 64, 2], P('nodes'), may hold values from 0 to 15
- nbr_slot: int32 [64, 128], P('nodes'), may hold values from 0 to 127, each once within a row
Outputs:
- activation: bfloat16 [256, 131072], P('feat', 'nodes')
- weight_grad: float32 [128, 256], P(None, 'feat')
- input_grad: float32 [128, 131072], P('feat', 'nodes')
Inputs may be any that keep to these rules, and one draw needn't show every extreme that they name: `nbr_slot`: each row is a permutation of 0 to 127: every received slot feeds exactly one tile. `hub_ids`: hub numbers may repeat.
All inputs are finite; a program needn't handle non-finite values.
Results may differ from a plain program's by a relative error of at most 0.0057.
Values may be sent and summed in bfloat16 or wider, within the bound.
No kernel may reach another device: no remote copies, remote signals or barrier semaphores. Data moves between devices by JAX's collectives and lax.ppermute only.
A program may use at most 64 MiB of HBM per device.

v0:
```python
import jax
import jax.numpy as jnp
from jax import lax
from jax.experimental import pallas as pl
from jax.experimental.pallas import tpu as pltpu
from jax.sharding import PartitionSpec as P

BF = jnp.bfloat16
F32 = jnp.float32


def silu_slope(pre):
    sig = jax.nn.sigmoid(pre)
    return sig * (1.0 + pre * (1.0 - sig))


def swap(values):
    return lax.all_to_all(values, "nodes", split_axis=0, concat_axis=0, tiled=True)


def trade(values, step):
    count = lax.axis_size("feat")
    return lax.ppermute(values, "feat", [(i, i ^ step) for i in range(count)])


def spread(piece, axes):
    count = 1
    for name in axes:
        count = count * lax.axis_size(name)
    pieces = jnp.broadcast_to(piece[None], (count,) + piece.shape)
    return lax.all_to_all(pieces, axes, split_axis=0, concat_axis=0, tiled=True)


TAIL = 8
SMEM = pl.BlockSpec(memory_space=pltpu.SMEM)
VMEM = pl.BlockSpec(memory_space=pltpu.VMEM)


def pack_kernel(numbers_ref, x_ref, msg_ref, tail_ref):
    quarter = x_ref.shape[0]
    count, rows, block_len = msg_ref.shape
    blk_count = x_ref.shape[1] // block_len
    per_dev = (rows - TAIL) // quarter
    hubs = numbers_ref.shape[0] - count * per_dev
    share = hubs * quarter // count

    def columns(block):
        return pl.ds(pl.multiple_of(block * block_len, block_len), block_len)

    def one(r, carry):
        for k in range(per_dev):
            block = numbers_ref[r * per_dev + k]
            msg_ref[r, k * quarter : (k + 1) * quarter, :] = x_ref[:, columns(block)]
        return carry

    lax.fori_loop(0, count, one, 0, unroll=8)
    tail_ref[...] = jnp.zeros_like(tail_ref)
    for h in range(hubs):
        local = numbers_ref[count * per_dev + h]
        inside = (local >= 0) & (local < blk_count)
        values = x_ref[:, columns(jnp.clip(local, 0, blk_count - 1))].astype(F32)
        values = jnp.where(inside, values, 0.0)
        for i in range(quarter // share):
            place = h * (quarter // share) + i
            tail_ref[place, :share, :] = values[i * share : (i + 1) * share]
    msg_ref[:, per_dev * quarter :, :] = tail_ref[...].astype(BF)


def pack(numbers, x_t, count, per_dev, block_len):
    rows = per_dev * x_t.shape[0] + TAIL
    return pl.pallas_call(
        pack_kernel,
        out_shape=jax.ShapeDtypeStruct((count, rows, block_len), BF),
        in_specs=[SMEM, VMEM],
        out_specs=VMEM,
        scratch_shapes=[pltpu.VMEM((count, TAIL, block_len), F32)],
        compiler_params=pltpu.CompilerParams(vmem_limit_bytes=48 << 20),
        name="pack",
    )(numbers, x_t)


def middle_kernel(row_ref, hub_ref, p0, p1, p2, p3, weight_ref, cot_ref, act_ref, out_ref):
    parts = (p0, p1, p2, p3)
    blks, quarter, block_len = p0.shape
    hid = weight_ref.shape[0] // len(parts)
    weight = weight_ref[...]
    total = jnp.zeros((weight.shape[0], weight.shape[1]), F32)
    for b in range(blks):
        columns = slice(b * block_len, (b + 1) * block_len)
        agg = []
        for k, part in enumerate(parts):
            first = pl.multiple_of((row_ref[0] ^ k) * quarter, quarter)
            agg.append(part[b].astype(F32) + hub_ref[b, pl.ds(first, quarter), :])
        agg = jnp.concatenate(agg, axis=0).astype(BF)
        pre = jnp.dot(weight, agg, preferred_element_type=F32)
        sig = jax.nn.sigmoid(pre)
        act_ref[:, columns] = (pre * sig).astype(BF)
        slope = sig * (1.0 + pre * (1.0 - sig))
        pre_grad = (cot_ref[:, columns].astype(F32) * slope).astype(BF)
        agg_grad = lax.dot_general(
            weight, pre_grad, (((0,), (0,)), ((), ())), preferred_element_type=F32
        ).astype(BF)
        for k in range(len(parts)):
            out_ref[k, b * quarter : (b + 1) * quarter, :] = agg_grad[k * quarter : (k + 1) * quarter]
        total = total + lax.dot_general(
            pre_grad, agg, (((1,), (1,)), ((), ())), preferred_element_type=F32
        )
    total = total.astype(BF)
    for k in range(len(parts)):
        out_ref[k, blks * quarter :, :] = total[k * hid : (k + 1) * hid]


def middle(row, hub_agg, parts, weight, cot):
    blks, quarter, block_len = parts[0].shape
    hid = weight.shape[0] // len(parts)
    return pl.pallas_call(
        middle_kernel,
        out_shape=[
            jax.ShapeDtypeStruct(cot.shape, BF),
            jax.ShapeDtypeStruct((len(parts), blks * quarter + hid, block_len), BF),
        ],
        in_specs=[SMEM] + [VMEM] * (3 + len(parts)),
        out_specs=[VMEM, VMEM],
        compiler_params=pltpu.CompilerParams(vmem_limit_bytes=16 << 20),
        cost_estimate=pl.CostEstimate(flops=6 * weight.size * cot.shape[1], transcendentals=cot.size, bytes_accessed=2 << 20),
        name="middle",
    )(row, hub_agg, *parts, weight, cot)


def finish_kernel(hubs_ref, own_ref, sums_ref, grad_ref, weight_ref, hub_ref):
    quarter = own_ref.shape[0]
    hubs, block_len = hub_ref.shape[0], hub_ref.shape[2]
    blk_count = own_ref.shape[1] // block_len
    count = sums_ref.shape[0]
    share = hubs * quarter // count
    for place in range(count):
        h, i = divmod(place, quarter // share)
        piece = sums_ref[place].astype(F32)
        hub_ref[h, i * share : (i + 1) * share, :] = piece[:share]
        weight_ref[place : place + 1, :] = piece[share : share + 1]
    grad_ref[...] = own_ref[...]
    for h in range(hubs):
        local = hubs_ref[h]

        @pl.when((local >= 0) & (local < blk_count))
        def _():
            first = jnp.clip(local, 0, blk_count - 1) * block_len
            columns = pl.ds(pl.multiple_of(first, block_len), block_len)
            grad_ref[:, columns] += hub_ref[h]


def finish(hubs_here, own, sums, quarter, hid, block_len):
    return pl.pallas_call(
        finish_kernel,
        out_shape=[
            jax.ShapeDtypeStruct(own.shape, F32),
            jax.ShapeDtypeStruct((hid, block_len), F32),
        ],
        in_specs=[SMEM, VMEM, VMEM],
        out_specs=[VMEM, VMEM],
        scratch_shapes=[pltpu.VMEM((hubs_here.shape[0], quarter, block_len), F32)],
        compiler_params=pltpu.CompilerParams(vmem_limit_bytes=16 << 20),
        name="finish",
    )(hubs_here, own, sums)


def per_device(
    x_t, weight, cotangent, self_tiles, hub_tiles, nbr_tiles, hub_ids, send_list, nbr_slot
):
    quarter = x_t.shape[0]
    blk_count, block_len = self_tiles.shape[0], self_tiles.shape[1]
    hubs, nbrs = hub_tiles.shape[1], nbr_tiles.shape[1]
    hid = weight.shape[1]
    count = lax.axis_size("nodes")
    feats = lax.axis_size("feat")
    row = lax.axis_index("feat")
    me = lax.axis_index("nodes")
    sends = send_list[0].reshape(-1)
    slots = nbr_slot[0]
    per_pair = 2 * quarter
    blk_share = blk_count // feats
    share = blk_share * block_len
    steps = jnp.arange(feats, dtype=jnp.int32)

    ids = jnp.arange(blk_count, dtype=jnp.int32)
    hubs_here = hub_ids - me * blk_count
    per_dev = send_list.shape[2]
    got = swap(pack(jnp.concatenate([sends, hubs_here]), x_t, count, per_dev, block_len))

    cot = cotangent.reshape(hid, feats, share)
    cot_parts, weight_parts = [], []
    for k in range(feats):
        part = lax.dynamic_index_in_dim(cot, row ^ k, 1, keepdims=False)
        part = jnp.concatenate([part, weight.T], axis=1)
        part = trade(part, k) if k else part
        cot_parts.append(part[:, :share])
        weight_parts.append(part[:, share:])
    cot_share = jnp.concatenate(cot_parts, axis=0)
    turned = jnp.concatenate(weight_parts, axis=0).reshape(feats * hid, feats, quarter)
    turned = jnp.take(turned, row ^ steps, axis=1, mode="clip")
    feat_ids = jnp.arange(feats * quarter, dtype=jnp.int32)
    owner = row ^ steps[:, None] ^ (feat_ids[None, :] // quarter)
    source = feat_ids[None, :] % quarter + owner * quarter
    unturn = (source[:, None, :] == feat_ids[None, :, None]).astype(BF)

    got, slots, sends, x_t, hubs_here, turned, cot_share, unturn = lax.optimization_barrier(
        (got, slots, sends, x_t, hubs_here, turned, cot_share, unturn)
    )
    blocks = x_t.reshape(quarter, blk_count, block_len).transpose(1, 0, 2)
    hub_rows = hubs * quarter // count
    hub_piece = jnp.sum(got[:, per_pair : per_pair + hub_rows].astype(F32), axis=0).astype(BF)
    hub_x = spread(hub_piece, ("nodes", "feat")).reshape(count, feats, hub_rows, block_len)
    hub_x = hub_x.transpose(1, 0, 2, 3).reshape(feats, hubs, quarter, block_len)

    slot_x = got[:, :per_pair].reshape(-1, quarter, block_len)
    chosen = jnp.take(slot_x, slots, axis=0, mode="clip")
    chosen = chosen.reshape(blk_count, nbrs, quarter, block_len)
    total = jnp.einsum("bjfs,bjsd->bfd", chosen, nbr_tiles, preferred_element_type=F32)
    total = total + jnp.einsum("bfs,bsd->bfd", blocks, self_tiles, preferred_element_type=F32)
    total = total.astype(BF).reshape(feats, blk_share, quarter, block_len)
    parts = []
    for k in range(feats):
        part = lax.dynamic_index_in_dim(total, row ^ k, 0, keepdims=False)
        parts.append(trade(part, k) if k else part)
    hub_share = lax.dynamic_slice_in_dim(hub_tiles, row * blk_share, blk_share, axis=0)
    hub_agg = jnp.einsum("ghfs,bhsd->bgfd", hub_x, hub_share, preferred_element_type=F32)
    hub_agg = hub_agg.reshape(blk_share, feats * quarter, block_len)
    act, message = middle(row.reshape(1), hub_agg, parts, turned.reshape(feats * hid, feats * quarter), cot_share)
    message = jnp.stack([message[0]] + [trade(message[k], k) for k in range(1, feats)])
    upstream = message[:, : blk_share * quarter].reshape(feats, blk_share, quarter, block_len)
    upstream = jnp.take(upstream, row ^ steps, axis=0, mode="clip")
    upstream = upstream.reshape(blk_count, quarter, block_len)
    weight_sum = jnp.einsum(
        "khe,kef->hf", message[:, blk_share * quarter :], unturn, preferred_element_type=F32
    )

    near = jnp.einsum("bfd,bjsd->bjfs", upstream, nbr_tiles, preferred_element_type=F32)
    near = near.astype(BF).reshape(blk_count * nbrs, quarter, block_len)
    tile_of = jnp.zeros_like(slots).at[slots].set(jnp.arange(slots.shape[0], dtype=slots.dtype))
    placed = jnp.take(near, tile_of, axis=0, mode="clip").reshape(count, per_pair, block_len)
    hub_terms = jnp.einsum("bfd,bhsd->hfs", upstream, hub_tiles, preferred_element_type=F32)
    hub_terms = hub_terms.astype(BF).reshape(count, -1, block_len)
    weight_sum = weight_sum.astype(BF).reshape(count, -1, block_len)
    back = swap(jnp.concatenate([placed, hub_terms, weight_sum], axis=1))

    act = act.reshape(feats, hid, share)
    acts = [act[0]] + [trade(act[k], k) for k in range(1, feats)]
    activation = jnp.take(jnp.stack(acts, axis=1), row ^ steps, axis=1, mode="clip")
    activation = activation.reshape(hid, blk_count * block_len)

    sums = jnp.sum(back[:, per_pair : per_pair + hub_rows + 1].astype(F32), axis=0)
    sums = spread(sums.astype(BF), ("nodes",))
    returned = back[:, :per_pair].reshape(-1, quarter, block_len)
    own = jnp.einsum("bfd,bsd->bfs", upstream, self_tiles, preferred_element_type=F32)
    send_select = (sends[:, None] == ids[None, :]).astype(BF)
    own = own + jnp.einsum("rfs,rb->bfs", returned, send_select, preferred_element_type=F32)
    own = own.transpose(1, 0, 2).reshape(quarter, blk_count * block_len)
    input_grad, weight_grad = finish(hubs_here, own, sums, quarter, hid, block_len)
    return (activation, weight_grad.T, input_grad)


def solution(mesh):
    return jax.shard_map(
        per_device,
        mesh=mesh,
        in_specs=(
            P("feat", "nodes"),
            P(None, "feat"),
            P("feat", "nodes"),
            P("nodes", None, None),
            P("nodes", None, None, None),
            P("nodes", None, None, None),
            P(),
            P("nodes", None, None),
            P("nodes", None),
        ),
        out_specs=(P("feat", "nodes"), P(None, "feat"), P("feat", "nodes")),
        check_vma=False,
    )
```

profile of v0, /device:TPU:1, one launch (start us, length us, event | category | flops | bytes accessed | tf_op | source)
XLA Modules:
  0.0 149.5 jit_solution(3288191099523251283)
XLA Ops:
  0.7 0.8 copy.37
  1.6 0.7 broadcast_subtract_fusion.hubs_ref
  2.3 0.9 copy-done.1
  3.2 2.0 %pack.1 = bf16[64,72,128]{2,1,0:T(8,128)(2,1)} custom-call(s32[136]{0:T(256)S(1)} %pad_add_fusion.numbers_ref, bf16[32,2048]{1,0:T(8,128)(2,1)S(1)} %copy-done.1), custom_call_target="tpu_custom_call" | custom-call | tf_op jit(solution)/shard_map/pack/pallas_call | solution.py:71
  5.2 13.1 %all-to-all-start = ((bf16[64,72,128]{2,1,0:T(8,128)(2,1)}), bf16[64,72,128]{2,1,0:T(8,128)(2,1)S(1)}, u32[]{:S(2)}, u32[]{:S(2)}) async-start(bf16[64,72,128]{2,1,0:T(8,128)(2,1)} %pack.1), calls=%async_computation | async-start | bytes 2359296 | tf_op jit(solution)/shard_map/all_to_all | solution.py:18
  18.5 0.6 constant_dynamic-slice_fusion
  19.2 1.4 collective-permute-start
  20.6 2.6 %collective-permute-start.1 = (bf16[64,640]{1,0:T(8,128)(2,1)S(1)}, bf16[64,640]{1,0:T(8,128)(2,1)S(1)}, u32[]{:S(2)}, u32[]{:S(2)}) collective-permute-start(bf16[64,640]{1,0:T(8,128)(2,1)S(1)} %get-tuple-element.44), channel_id=1, source_target_pairs={{0,2},{1,3},{2,0},{3,1},{4,6},{5,7},{6,4},{7,5},{8,10},{9,11},{10,... | collective-permute-start | bytes 245768 | tf_op jit(solution)/shard_map/ppermute | solution.py:23
  23.3 0.7 fusion.10
  24.0 3.0 %collective-permute-done.1 = bf16[64,640]{1,0:T(8,128)(2,1)S(1)} collective-permute-done((bf16[64,640]{1,0:T(8,128)(2,1)S(1)}, bf16[64,640]{1,0:T(8,128)(2,1)S(1)}, u32[]{:S(2)}, u32[]{:S(2)}) %collective-permute-start.1) | collective-permute-done | bytes 81952 | tf_op jit(solution)/shard_map/ppermute | solution.py:23
  27.0 1.9 %collective-permute-done.2 = bf16[64,640]{1,0:T(8,128)(2,1)S(1)} collective-permute-done((bf16[64,640]{1,0:T(8,128)(2,1)S(1)}, bf16[64,640]{1,0:T(8,128)(2,1)S(1)}, u32[]{:S(2)}, u32[]{:S(2)}) %collective-permute-start.2) | collective-permute-done | bytes 81952 | tf_op jit(solution)/shard_map/ppermute | solution.py:23
  29.1 0.6 gather_fusion
  29.7 19.9 %all-to-all-done = bf16[64,72,128]{2,1,0:T(8,128)(2,1)S(1)} async-done(((bf16[64,72,128]{2,1,0:T(8,128)(2,1)}), bf16[64,72,128]{2,1,0:T(8,128)(2,1)S(1)}, u32[]{:S(2)}, u32[]{:S(2)}) %all-to-all-start) | async-done | bytes 1179680 | tf_op jit(solution)/shard_map/all_to_all | solution.py:18
  50.0 0.8 broadcast_in_dim.19
  50.8 8.9 %all-to-all-start.1 = ((bf16[256,4,128]{2,1,0:T(4,128)(2,1)}), bf16[256,4,128]{2,1,0:T(4,128)(2,1)S(1)}, u32[]{:S(2)}, u32[]{:S(2)}) async-start(bf16[256,4,128]{2,1,0:T(4,128)(2,1)} %broadcast_in_dim.19), calls=%async_computation.1 | async-start | bytes 524288 | tf_op jit(solution)/shard_map/all_to_all | solution.py:31
  59.7 0.8 gather_fusion.1
  60.4 3.0 %convolution_bitcast_fusion = f32[16,32,128]{2,1,0:T(8,128)S(1)} fusion(bf16[16,8,32,128]{3,2,1,0:T(8,128)(2,1)S(1)} %bitcast.131, bf16[16,8,128,128]{3,2,1,0:T(8,128)(2,1)} %param.14), kind=kOutput, calls=%fused_computation.11 | convolution fusion | flops 134217728 | bytes 5505024 | tf_op jit(solution)/shard_map/bjfs,bjsd->bfd/dot_general | solution.py:218
  63.7 2.7 %collective-permute-start.5 = (bf16[4,32,128]{2,1,0:T(8,128)(2,1)S(1)}, bf16[4,32,128]{2,1,0:T(8,128)(2,1)S(1)}, u32[]{:S(2)}, u32[]{:S(2)}) collective-permute-start(bf16[4,32,128]{2,1,0:T(8,128)(2,1)S(1)} %get-tuple-element.39), channel_id=1, source_target_pairs={{0,3},{1,2},{2,1},{3,0},{4,7},{5,6},{6,5},{7,4},{8,11},{9,10},{10,... | collective-permute-start | bytes 98312 | tf_op jit(solution)/shard_map/ppermute | solution.py:23
  66.5 0.5 collective-permute-start.4
  67.1 1.0 scatter_custom_fusion
  68.1 7.2 %all-to-all-done.1 = bf16[256,4,128]{2,1,0:T(4,128)(2,1)S(1)} async-done(((bf16[256,4,128]{2,1,0:T(4,128)(2,1)}), bf16[256,4,128]{2,1,0:T(4,128)(2,1)S(1)}, u32[]{:S(2)}, u32[]{:S(2)}) %all-to-all-start.1) | async-done | bytes 262176 | tf_op jit(solution)/shard_map/all_to_all | solution.py:31
  75.6 1.5 %fusion.5 = f32[4,128,4,32,1]{1,3,4,2,0:T(8,128)S(1)} fusion(bf16[4,8,32,128,1]{3,2,1,0,4:T(8,128)(2,1)S(1)} %bitcast.148, bf16[16,8,128,128]{3,2,1,0:T(8,128)(2,1)} %param.13, s32[]{:T(128)S(6)} %select_n.46), kind=kOutput, calls=%fused_computation.18 | convolution fusion | flops 134217728 | bytes 1572868 | tf_op jit(solution)/shard_map/ghfs,bhsd->bgfd/dot_general | solution.py:226
  77.2 0.9 middle.1
  78.4 1.8 %collective-permute-start.10 = (bf16[192,128]{1,0:T(8,128)(2,1)S(1)}, bf16[192,128]{1,0:T(8,128)(2,1)S(1)}, u32[]{:S(2)}, u32[]{:S(2)}) collective-permute-start(bf16[192,128]{1,0:T(8,128)(2,1)S(1)} %get-tuple-element.37), channel_id=1, source_target_pairs={{0,2},{1,3},{2,0},{3,1},{4,6},{5,7},{6,4},{7,5},{8,10},{9,11},{10,... | collective-permute-start | bytes 147464 | tf_op jit(solution)/shard_map/ppermute | solution.py:23
  80.3 1.2 collective-permute-start.9
  81.5 0.9 collective-permute-done.11
  82.4 0.5 collective-permute-done.10
  82.9 0.9 collective-permute-done.9
  83.8 0.6 gather_fusion.3
  84.4 3.6 %fusion.2 = bf16[32,8,128]{2,0,1:T(8,128)(2,1)S(1)} fusion(bf16[16,32,128,1]{2,1,3,0:T(8,128)(2,1)S(1)} %bitcast.136, bf16[16,8,128,128]{3,2,1,0:T(8,128)(2,1)} %param.13), kind=kOutput, calls=%fused_computation.14 | convolution fusion | flops 134250496 | bytes 4390912 | tf_op jit(solution)/shard_map/bfd,bhsd->hfs/dot_general | solution.py:241
  88.1 1.5 %convolution_convert_fusion = bf16[16,32,8,128]{3,1,2,0:T(8,128)(2,1)S(1)} fusion(bf16[16,32,128,1]{2,1,3,0:T(8,128)(2,1)S(1)} %bitcast.137, bf16[16,8,128,128]{3,2,1,0:T(8,128)(2,1)S(1)} %copy-done.3), kind=kOutput, calls=%fused_computation.6 | convolution fusion | flops 134742016 | bytes 5373952 | tf_op jit(solution)/shard_map/bfd,bjsd->bjfs/dot_general | solution.py:237
  89.8 0.8 gather_fusion.4
  90.6 1.2 pad_maximum_fusion
  91.8 7.6 %all-to-all-start.2 = ((bf16[64,69,128]{2,1,0:T(8,128)(2,1)}), bf16[64,69,128]{2,1,0:T(8,128)(2,1)S(1)}, u32[]{:S(2)}, u32[]{:S(2)}) async-start(bf16[64,69,128]{2,1,0:T(8,128)(2,1)} %pad_maximum_fusion), calls=%async_computation.2 | async-start | bytes 2359296 | tf_op jit(solution)/shard_map/all_to_all | solution.py:18
  99.5 1.5 %collective-permute-start.8 = (bf16[64,512]{1,0:T(8,128)(2,1)S(1)}, bf16[64,512]{1,0:T(8,128)(2,1)S(1)}, u32[]{:S(2)}, u32[]{:S(2)}) collective-permute-start(bf16[64,512]{1,0:T(8,128)(2,1)S(1)} %get-tuple-element.28), channel_id=1, source_target_pairs={{0,3},{1,2},{2,1},{3,0},{4,7},{5,6},{6,5},{7,4},{8,11},{9,10},{10,... | collective-permute-start | bytes 196616 | tf_op jit(solution)/shard_map/ppermute | solution.py:23
  101.0 1.1 collective-permute-start.7
  102.1 0.7 collective-permute-start.6
  102.8 1.4 collective-permute-done.8
  104.2 1.4 collective-permute-done.7
  106.0 0.6 gather_fusion.2
  106.5 0.7 copy.63
  107.3 23.5 %all-to-all-done.2 = bf16[64,69,128]{2,1,0:T(8,128)(2,1)S(1)} async-done(((bf16[64,69,128]{2,1,0:T(8,128)(2,1)}), bf16[64,69,128]{2,1,0:T(8,128)(2,1)S(1)}, u32[]{:S(2)}, u32[]{:S(2)}) %all-to-all-start.2) | async-done | bytes 1130528 | tf_op jit(solution)/shard_map/all_to_all | solution.py:18
  130.9 0.7 broadcast_in_dim.23
  131.5 6.2 %all-to-all-start.3 = ((bf16[64,5,128]{2,1,0:T(8,128)(2,1)}), bf16[64,5,128]{2,1,0:T(8,128)(2,1)S(1)}, u32[]{:S(2)}, u32[]{:S(2)}) async-start(bf16[64,5,128]{2,1,0:T(8,128)(2,1)} %broadcast_in_dim.23), calls=%async_computation.3 | async-start | bytes 262144 | tf_op jit(solution)/shard_map/all_to_all | solution.py:31
  137.9 0.4 fusion.7
  138.3 0.4 fusion
  138.7 9.4 %all-to-all-done.3.sums_ref = bf16[64,5,128]{2,1,0:T(8,128)(2,1)S(1)} async-done(((bf16[64,5,128]{2,1,0:T(8,128)(2,1)}), bf16[64,5,128]{2,1,0:T(8,128)(2,1)S(1)}, u32[]{:S(2)}, u32[]{:S(2)}) %all-to-all-start.3) | async-done | bytes 81952 | tf_op jit(solution)/shard_map/all_to_all | solution.py:31
  148.1 1.4 finish.1
  (65 shorter events, 2.9 us)
Async XLA Ops:
  0.6 62.8 %copy-start = (bf16[16,128,128]{2,1,0:T(8,128)(2,1)S(1)}, bf16[16,128,128]{2,1,0:T(8,128)(2,1)}, u32[]{:S(2)}) copy-start(bf16[16,128,128]{2,1,0:T(8,128)(2,1)} %param.12) | copy-start | bytes 1572868
  2.3 0.9 copy-start.1
  3.2 15.1 %copy-start.5 = (bf16[64,2048]{1,0:T(8,128)(2,1)S(1)}, bf16[64,2048]{1,0:T(8,128)(2,1)}, u32[]{:S(2)}) copy-start(bf16[64,2048]{1,0:T(8,128)(2,1)} %param.11) | copy-start | bytes 786436
  5.2 14.0 %copy-start.6 = (bf16[128,64]{0,1:T(8,128)(2,1)S(1)}, bf16[128,64]{0,1:T(8,128)(2,1)}, u32[]{:S(2)}) copy-start(bf16[128,64]{0,1:T(8,128)(2,1)} %param.10) | copy-start | bytes 49156
  5.2 44.5 %all-to-all-start = ((bf16[64,72,128]{2,1,0:T(8,128)(2,1)}), bf16[64,72,128]{2,1,0:T(8,128)(2,1)S(1)}, u32[]{:S(2)}, u32[]{:S(2)}) async-start(bf16[64,72,128]{2,1,0:T(8,128)(2,1)} %pack.1), calls=%async_computation | async-start | bytes 2359296 | tf_op jit(solution)/shard_map/all_to_all | solution.py:18
  19.1 30.9 %copy-start.7 = (s32[1,128]{1,0:T(1,128)S(1)}, s32[1,128]{1,0:T(1,128)}, u32[]{:S(2)}) copy-start(s32[1,128]{1,0:T(1,128)} %param.17) | copy-start | bytes 1540
  19.2 4.8 %collective-permute-start = (bf16[64,640]{1,0:T(8,128)(2,1)S(1)}, bf16[64,640]{1,0:T(8,128)(2,1)S(1)}, u32[]{:S(2)}, u32[]{:S(2)}) collective-permute-start(bf16[64,640]{1,0:T(8,128)(2,1)S(1)} %get-tuple-element.43), channel_id=1, source_target_pairs={{0,1},{1,0},{2,3},{3,2},{4,5},{5,4},{6,7},{7,6},{8,9},{9,8},{10,11... | collective-permute-start | bytes 245768 | tf_op jit(solution)/shard_map/ppermute | solution.py:23
  20.6 6.5 %collective-permute-start.1 = (bf16[64,640]{1,0:T(8,128)(2,1)S(1)}, bf16[64,640]{1,0:T(8,128)(2,1)S(1)}, u32[]{:S(2)}, u32[]{:S(2)}) collective-permute-start(bf16[64,640]{1,0:T(8,128)(2,1)S(1)} %get-tuple-element.44), channel_id=1, source_target_pairs={{0,2},{1,3},{2,0},{3,1},{4,6},{5,7},{6,4},{7,5},{8,10},{9,11},{10,... | collective-permute-start | bytes 245768 | tf_op jit(solution)/shard_map/ppermute | solution.py:23
  23.2 5.8 %collective-permute-start.2 = (bf16[64,640]{1,0:T(8,128)(2,1)S(1)}, bf16[64,640]{1,0:T(8,128)(2,1)S(1)}, u32[]{:S(2)}, u32[]{:S(2)}) collective-permute-start(bf16[64,640]{1,0:T(8,128)(2,1)S(1)} %get-tuple-element.45), channel_id=1, source_target_pairs={{0,3},{1,2},{2,1},{3,0},{4,7},{5,6},{6,5},{7,4},{8,11},{9,10},{10,... | collective-permute-start | bytes 245768 | tf_op jit(solution)/shard_map/ppermute | solution.py:23
  50.8 24.6 %all-to-all-start.1 = ((bf16[256,4,128]{2,1,0:T(4,128)(2,1)}), bf16[256,4,128]{2,1,0:T(4,128)(2,1)S(1)}, u32[]{:S(2)}, u32[]{:S(2)}) async-start(bf16[256,4,128]{2,1,0:T(4,128)(2,1)} %broadcast_in_dim.19), calls=%async_computation.1 | async-start | bytes 524288 | tf_op jit(solution)/shard_map/all_to_all | solution.py:31
  60.4 3.0 %copy-start.2 = (bf16[32,2048]{1,0:T(8,128)(2,1)S(1)}, bf16[32,2048]{1,0:T(8,128)(2,1)}, u32[]{:S(2)}) copy-start(bf16[32,2048]{1,0:T(8,128)(2,1)} %x_ref.1) | copy-start | bytes 393220
  63.7 13.4 %collective-permute-start.5 = (bf16[4,32,128]{2,1,0:T(8,128)(2,1)S(1)}, bf16[4,32,128]{2,1,0:T(8,128)(2,1)S(1)}, u32[]{:S(2)}, u32[]{:S(2)}) collective-permute-start(bf16[4,32,128]{2,1,0:T(8,128)(2,1)S(1)} %get-tuple-element.39), channel_id=1, source_target_pairs={{0,3},{1,2},{2,1},{3,0},{4,7},{5,6},{6,5},{7,4},{8,11},{9,10},{10,... | collective-permute-start | bytes 98312 | tf_op jit(solution)/shard_map/ppermute | solution.py:23
  66.5 10.7 %collective-permute-start.4 = (bf16[4,32,128]{2,1,0:T(8,128)(2,1)S(1)}, bf16[4,32,128]{2,1,0:T(8,128)(2,1)S(1)}, u32[]{:S(2)}, u32[]{:S(2)}) collective-permute-start(bf16[4,32,128]{2,1,0:T(8,128)(2,1)S(1)} %get-tuple-element.40), channel_id=1, source_target_pairs={{0,2},{1,3},{2,0},{3,1},{4,6},{5,7},{6,4},{7,5},{8,10},{9,11},{10,... | collective-permute-start | bytes 98312 | tf_op jit(solution)/shard_map/ppermute | solution.py:23
  67.0 10.2 %collective-permute-start.3 = (bf16[4,32,128]{2,1,0:T(8,128)(2,1)S(1)}, bf16[4,32,128]{2,1,0:T(8,128)(2,1)S(1)}, u32[]{:S(2)}, u32[]{:S(2)}) collective-permute-start(bf16[4,32,128]{2,1,0:T(8,128)(2,1)S(1)} %get-tuple-element.41), channel_id=1, source_target_pairs={{0,1},{1,0},{2,3},{3,2},{4,5},{5,4},{6,7},{7,6},{8,9},{9,8},{10,11... | collective-permute-start | bytes 98312 | tf_op jit(solution)/shard_map/ppermute | solution.py:23
  78.1 4.2 %collective-permute-start.11 = (bf16[192,128]{1,0:T(8,128)(2,1)S(1)}, bf16[192,128]{1,0:T(8,128)(2,1)S(1)}, u32[]{:S(2)}, u32[]{:S(2)}) collective-permute-start(bf16[192,128]{1,0:T(8,128)(2,1)S(1)} %get-tuple-element.36), channel_id=1, source_target_pairs={{0,3},{1,2},{2,1},{3,0},{4,7},{5,6},{6,5},{7,4},{8,11},{9,10},{10,... | collective-permute-start | bytes 147464 | tf_op jit(solution)/shard_map/ppermute | solution.py:23
  78.4 4.4 %collective-permute-start.10 = (bf16[192,128]{1,0:T(8,128)(2,1)S(1)}, bf16[192,128]{1,0:T(8,128)(2,1)S(1)}, u32[]{:S(2)}, u32[]{:S(2)}) collective-permute-start(bf16[192,128]{1,0:T(8,128)(2,1)S(1)} %get-tuple-element.37), channel_id=1, source_target_pairs={{0,2},{1,3},{2,0},{3,1},{4,6},{5,7},{6,4},{7,5},{8,10},{9,11},{10,... | collective-permute-start | bytes 147464 | tf_op jit(solution)/shard_map/ppermute | solution.py:23
  80.3 3.5 %collective-permute-start.9 = (bf16[192,128]{1,0:T(8,128)(2,1)S(1)}, bf16[192,128]{1,0:T(8,128)(2,1)S(1)}, u32[]{:S(2)}, u32[]{:S(2)}) collective-permute-start(bf16[192,128]{1,0:T(8,128)(2,1)S(1)} %get-tuple-element.38), channel_id=1, source_target_pairs={{0,1},{1,0},{2,3},{3,2},{4,5},{5,4},{6,7},{7,6},{8,9},{9,8},{10,11... | collective-permute-start | bytes 147464 | tf_op jit(solution)/shard_map/ppermute | solution.py:23
  84.4 3.7 %copy-start.3 = (bf16[16,8,128,128]{3,2,1,0:T(8,128)(2,1)S(1)}, bf16[16,8,128,128]{3,2,1,0:T(8,128)(2,1)}, u32[]{:S(2)}) copy-start(bf16[16,8,128,128]{3,2,1,0:T(8,128)(2,1)} %param.14) | copy-start | bytes 12582916
  88.1 1.6 %copy-start.4 = (bf16[4,128,128]{2,1,0:T(8,128)(2,1)S(1)}, bf16[4,128,128]{2,1,0:T(8,128)(2,1)}, u32[]{:S(2)}) copy-start(bf16[4,128,128]{2,1,0:T(8,128)(2,1)} %fusion.10) | copy-start | bytes 393220
  91.8 39.0 %all-to-all-start.2 = ((bf16[64,69,128]{2,1,0:T(8,128)(2,1)}), bf16[64,69,128]{2,1,0:T(8,128)(2,1)S(1)}, u32[]{:S(2)}, u32[]{:S(2)}) async-start(bf16[64,69,128]{2,1,0:T(8,128)(2,1)} %pad_maximum_fusion), calls=%async_computation.2 | async-start | bytes 2359296 | tf_op jit(solution)/shard_map/all_to_all | solution.py:18
  99.5 4.7 %collective-permute-start.8 = (bf16[64,512]{1,0:T(8,128)(2,1)S(1)}, bf16[64,512]{1,0:T(8,128)(2,1)S(1)}, u32[]{:S(2)}, u32[]{:S(2)}) collective-permute-start(bf16[64,512]{1,0:T(8,128)(2,1)S(1)} %get-tuple-element.28), channel_id=1, source_target_pairs={{0,3},{1,2},{2,1},{3,0},{4,7},{5,6},{6,5},{7,4},{8,11},{9,10},{10,... | collective-permute-start | bytes 196616 | tf_op jit(solution)/shard_map/ppermute | solution.py:23
  101.0 4.6 %collective-permute-start.7 = (bf16[64,512]{1,0:T(8,128)(2,1)S(1)}, bf16[64,512]{1,0:T(8,128)(2,1)S(1)}, u32[]{:S(2)}, u32[]{:S(2)}) collective-permute-start(bf16[64,512]{1,0:T(8,128)(2,1)S(1)} %get-tuple-element.29), channel_id=1, source_target_pairs={{0,2},{1,3},{2,0},{3,1},{4,6},{5,7},{6,4},{7,5},{8,10},{9,11},{10,... | collective-permute-start | bytes 196616 | tf_op jit(solution)/shard_map/ppermute | solution.py:23
  102.1 3.8 %collective-permute-start.6 = (bf16[64,512]{1,0:T(8,128)(2,1)S(1)}, bf16[64,512]{1,0:T(8,128)(2,1)S(1)}, u32[]{:S(2)}, u32[]{:S(2)}) collective-permute-start(bf16[64,512]{1,0:T(8,128)(2,1)S(1)} %get-tuple-element.30), channel_id=1, source_target_pairs={{0,1},{1,0},{2,3},{3,2},{4,5},{5,4},{6,7},{7,6},{8,9},{9,8},{10,11... | collective-permute-start | bytes 196616 | tf_op jit(solution)/shard_map/ppermute | solution.py:23
  131.5 16.6 %all-to-all-start.3 = ((bf16[64,5,128]{2,1,0:T(8,128)(2,1)}), bf16[64,5,128]{2,1,0:T(8,128)(2,1)S(1)}, u32[]{:S(2)}, u32[]{:S(2)}) async-start(bf16[64,5,128]{2,1,0:T(8,128)(2,1)} %broadcast_in_dim.23), calls=%async_computation.3 | async-start | bytes 262144 | tf_op jit(solution)/shard_map/all_to_all | solution.py:31
where the time goes:
time: 150 us; the launch traced here: 149 us
  waiting for transfers between devices  70.5 us (47%)
  starting transfers between devices  49.9 us (33%)
  matrix products  10.9 us (7%)
  local copies, waits for them, and re-layouts  9.94 us (7%)
  Pallas kernels  4.21 us (3%)
  other arithmetic  2.94 us (2%)
    all_to_all x2, waiting for transfers between devices, swap(): lax.all_to_all(values, 'nodes', split_axis=0, concat_axis=0, tiled=True)  43.4 us
    all_to_all x2, starting transfers between devices, swap(): lax.all_to_all(values, 'nodes', split_axis=0, concat_axis=0, tiled=True)  20.7 us
    all_to_all x2, waiting for transfers between devices, spread(): return lax.all_to_all(pieces, axes, split_axis=0, concat_axis=0, tiled=True)  16.6 us
    all_to_all x2, starting transfers between devices, spread(): return lax.all_to_all(pieces, axes, split_axis=0, concat_axis=0, tiled=True)  15 us
    ppermute x12, starting transfers between devices, trade(): return lax.ppermute(values, 'feat', [(i, i ^ step) for i in range(count)])  14.1 us
    ppermute x12, waiting for transfers between devices, trade(): return lax.ppermute(values, 'feat', [(i, i ^ step) for i in range(count)])  10.4 us
    dot_general x1, matrix products, per_device(): jnp.einsum('bfd,bhsd->hfs', upstream, hub_tiles, preferred_element_type=F32)  3.64 us
  transfers between devices with their start and end apart: 16, of which 12 were waited for; matrix products, arithmetic and copies ran while one was open for 8% of the time, Pallas kernels for 0%

commit v1 on v0

--- a/solution.py
+++ b/solution.py
@@ -36,12 +36,15 @@
 VMEM = pl.BlockSpec(memory_space=pltpu.VMEM)
 
 
-def pack_kernel(numbers_ref, x_ref, msg_ref, tail_ref):
+def pack_kernel(sends_ref, hubs_ref, x_hbm, msg_ref, x_ref, tail_ref, sem):
+    load = pltpu.make_async_copy(x_hbm, x_ref, sem)
+    load.start()
+    me = lax.axis_index("nodes")
     quarter = x_ref.shape[0]
     count, rows, block_len = msg_ref.shape
     blk_count = x_ref.shape[1] // block_len
     per_dev = (rows - TAIL) // quarter
-    hubs = numbers_ref.shape[0] - count * per_dev
+    hubs = hubs_ref.shape[0]
     share = hubs * quarter // count
 
     def columns(block):
@@ -49,14 +52,15 @@
 
     def one(r, carry):
         for k in range(per_dev):
-            block = numbers_ref[r * per_dev + k]
+            block = sends_ref[k, r]
             msg_ref[r, k * quarter : (k + 1) * quarter, :] = x_ref[:, columns(block)]
         return carry
 
+    tail_ref[...] = jnp.zeros_like(tail_ref)
+    load.wait()
     lax.fori_loop(0, count, one, 0, unroll=8)
-    tail_ref[...] = jnp.zeros_like(tail_ref)
     for h in range(hubs):
-        local = numbers_ref[count * per_dev + h]
+        local = hubs_ref[h] - me * blk_count
         inside = (local >= 0) & (local < blk_count)
         values = x_ref[:, columns(jnp.clip(local, 0, blk_count - 1))].astype(F32)
         values = jnp.where(inside, values, 0.0)
@@ -66,17 +70,21 @@
     msg_ref[:, per_dev * quarter :, :] = tail_ref[...].astype(BF)
 
 
-def pack(numbers, x_t, count, per_dev, block_len):
+def pack(sends, hub_ids, x_t, count, per_dev, block_len):
     rows = per_dev * x_t.shape[0] + TAIL
     return pl.pallas_call(
         pack_kernel,
         out_shape=jax.ShapeDtypeStruct((count, rows, block_len), BF),
-        in_specs=[SMEM, VMEM],
+        in_specs=[SMEM, SMEM, pl.BlockSpec(memory_space=pl.ANY)],
         out_specs=VMEM,
-        scratch_shapes=[pltpu.VMEM((count, TAIL, block_len), F32)],
-        compiler_params=pltpu.CompilerParams(vmem_limit_bytes=48 << 20),
+        scratch_shapes=[
+            pltpu.VMEM(x_t.shape, x_t.dtype),
+            pltpu.VMEM((count, TAIL, block_len), F32),
+            pltpu.SemaphoreType.DMA,
+        ],
+        compiler_params=pltpu.CompilerParams(vmem_limit_bytes=56 << 20),
         name="pack",
-    )(numbers, x_t)
+    )(sends, hub_ids, x_t)
 
 
 def middle_kernel(row_ref, hub_ref, p0, p1, p2, p3, weight_ref, cot_ref, act_ref, out_ref):
@@ -185,7 +193,7 @@
     ids = jnp.arange(blk_count, dtype=jnp.int32)
     hubs_here = hub_ids - me * blk_count
     per_dev = send_list.shape[2]
-    got = swap(pack(jnp.concatenate([sends, hubs_here]), x_t, count, per_dev, block_len))
+    got = swap(pack(send_list[0].T, hub_ids, x_t, count, per_dev, block_len))
 
     cot = cotangent.reshape(hid, feats, share)
     cot_parts, weight_parts = [], []

time: 150 us -> 149 us (level)
  local copies, waits for them, and re-layouts: 9.94 us -> 8.32 us
    unnamed x19, local copies, waits for them, and re-layouts: 1.81 us -> 0.19 us
  transfers between devices with their start and end apart: 16 -> 16, of which waited for: 12 -> 12; matrix products, arithmetic and copies ran while one was open for 8% -> 7% of each run, Pallas kernels for 0% -> 0%
where the time goes in v1:
time: 149 us; the launch traced here: 148 us
  waiting for transfers between devices  70.8 us (48%)
  starting transfers between devices  49.9 us (33%)
  matrix products  10.9 us (7%)
  local copies, waits for them, and re-layouts  8.32 us (6%)
  Pallas kernels  5.39 us (4%)
  other arithmetic  1.63 us (1%)
    all_to_all x2, waiting for transfers between devices, swap(): lax.all_to_all(values, 'nodes', split_axis=0, concat_axis=0, tiled=True)  43.5 us
    all_to_all x2, starting transfers between devices, swap(): lax.all_to_all(values, 'nodes', split_axis=0, concat_axis=0, tiled=True)  20.7 us
    all_to_all x2, waiting for transfers between devices, spread(): return lax.all_to_all(pieces, axes, split_axis=0, concat_axis=0, tiled=True)  16.6 us
    all_to_all x2, starting transfers between devices, spread(): return lax.all_to_all(pieces, axes, split_axis=0, concat_axis=0, tiled=True)  15 us
    ppermute x12, starting transfers between devices, trade(): return lax.ppermute(values, 'feat', [(i, i ^ step) for i in range(count)])  14.1 us
    ppermute x12, waiting for transfers between devices, trade(): return lax.ppermute(values, 'feat', [(i, i ^ step) for i in range(count)])  10.7 us
    dot_general x1, matrix products, per_device(): jnp.einsum('bfd,bhsd->hfs', upstream, hub_tiles, preferred_element_type=F32)  3.64 us
    pallas_call x1, Pallas kernels, pack(): pl.pallas_call(pack_kernel, out_shape=jax.ShapeDtypeStruct((count, rows,...  3.14 us
  transfers between devices with their start and end apart: 16, of which 12 were waited for; matrix products, arithmetic and copies ran while one was open for 7% of the time, Pallas kernels for 0%

profile of v1, /device:TPU:1, one launch (start us, length us, event | category | flops | bytes accessed | tf_op | source)
XLA Modules:
  0.0 148.1 jit_solution(16434283447176610981)
XLA Ops:
  0.7 3.1 %pack.1 = bf16[64,72,128]{2,1,0:T(8,128)(2,1)} custom-call(s32[2,64]{1,0:T(2,128)} %bitcast.164, s32[8]{0:T(128)} %hubs_ref.1, bf16[32,2048]{1,0:T(8,128)(2,1)} %x_hbm.1), custom_call_target="tpu_custom_call" | custom-call | tf_op jit(solution)/shard_map/pack/pallas_call | solution.py:75
  3.8 13.1 %all-to-all-start = ((bf16[64,72,128]{2,1,0:T(8,128)(2,1)}), bf16[64,72,128]{2,1,0:T(8,128)(2,1)S(1)}, u32[]{:S(2)}, u32[]{:S(2)}) async-start(bf16[64,72,128]{2,1,0:T(8,128)(2,1)} %pack.1), calls=%async_computation | async-start | bytes 2359296 | tf_op jit(solution)/shard_map/all_to_all | solution.py:18
  17.2 0.6 constant_dynamic-slice_fusion
  17.9 1.4 collective-permute-start
  19.3 2.6 %collective-permute-start.1 = (bf16[64,640]{1,0:T(8,128)(2,1)S(1)}, bf16[64,640]{1,0:T(8,128)(2,1)S(1)}, u32[]{:S(2)}, u32[]{:S(2)}) collective-permute-start(bf16[64,640]{1,0:T(8,128)(2,1)S(1)} %get-tuple-element.44), channel_id=1, source_target_pairs={{0,2},{1,3},{2,0},{3,1},{4,6},{5,7},{6,4},{7,5},{8,10},{9,11},{10,... | collective-permute-start | bytes 245768 | tf_op jit(solution)/shard_map/ppermute | solution.py:23
  22.3 3.4 %collective-permute-done.1 = bf16[64,640]{1,0:T(8,128)(2,1)S(1)} collective-permute-done((bf16[64,640]{1,0:T(8,128)(2,1)S(1)}, bf16[64,640]{1,0:T(8,128)(2,1)S(1)}, u32[]{:S(2)}, u32[]{:S(2)}) %collective-permute-start.1) | collective-permute-done | bytes 81952 | tf_op jit(solution)/shard_map/ppermute | solution.py:23
  25.7 1.9 %collective-permute-done.2 = bf16[64,640]{1,0:T(8,128)(2,1)S(1)} collective-permute-done((bf16[64,640]{1,0:T(8,128)(2,1)S(1)}, bf16[64,640]{1,0:T(8,128)(2,1)S(1)}, u32[]{:S(2)}, u32[]{:S(2)}) %collective-permute-start.2) | collective-permute-done | bytes 81952 | tf_op jit(solution)/shard_map/ppermute | solution.py:23
  27.8 0.6 gather_fusion
  28.4 19.9 %all-to-all-done = bf16[64,72,128]{2,1,0:T(8,128)(2,1)S(1)} async-done(((bf16[64,72,128]{2,1,0:T(8,128)(2,1)}), bf16[64,72,128]{2,1,0:T(8,128)(2,1)S(1)}, u32[]{:S(2)}, u32[]{:S(2)}) %all-to-all-start) | async-done | bytes 1179680 | tf_op jit(solution)/shard_map/all_to_all | solution.py:18
  48.7 0.8 broadcast_in_dim.19
  49.5 8.9 %all-to-all-start.1 = ((bf16[256,4,128]{2,1,0:T(4,128)(2,1)}), bf16[256,4,128]{2,1,0:T(4,128)(2,1)S(1)}, u32[]{:S(2)}, u32[]{:S(2)}) async-start(bf16[256,4,128]{2,1,0:T(4,128)(2,1)} %broadcast_in_dim.19), calls=%async_computation.1 | async-start | bytes 524288 | tf_op jit(solution)/shard_map/all_to_all | solution.py:31
  58.4 0.8 gather_fusion.1
  59.1 3.0 %convolution_bitcast_fusion = f32[16,32,128]{2,1,0:T(8,128)S(1)} fusion(bf16[16,8,32,128]{3,2,1,0:T(8,128)(2,1)S(1)} %bitcast.134, bf16[16,8,128,128]{3,2,1,0:T(8,128)(2,1)} %param.14), kind=kOutput, calls=%fused_computation.11 | convolution fusion | flops 134217728 | bytes 5505024 | tf_op jit(solution)/shard_map/bjfs,bjsd->bfd/dot_general | solution.py:226
  62.1 0.3 fusion.1
  62.4 2.7 %collective-permute-start.5 = (bf16[4,32,128]{2,1,0:T(8,128)(2,1)S(1)}, bf16[4,32,128]{2,1,0:T(8,128)(2,1)S(1)}, u32[]{:S(2)}, u32[]{:S(2)}) collective-permute-start(bf16[4,32,128]{2,1,0:T(8,128)(2,1)S(1)} %get-tuple-element.39), channel_id=1, source_target_pairs={{0,3},{1,2},{2,1},{3,0},{4,7},{5,6},{6,5},{7,4},{8,11},{9,10},{10,... | collective-permute-start | bytes 98312 | tf_op jit(solution)/shard_map/ppermute | solution.py:23
  65.2 0.5 collective-permute-start.4
  65.8 1.0 scatter_custom_fusion
  66.8 7.2 %all-to-all-done.1 = bf16[256,4,128]{2,1,0:T(4,128)(2,1)S(1)} async-done(((bf16[256,4,128]{2,1,0:T(4,128)(2,1)}), bf16[256,4,128]{2,1,0:T(4,128)(2,1)S(1)}, u32[]{:S(2)}, u32[]{:S(2)}) %all-to-all-start.1) | async-done | bytes 262176 | tf_op jit(solution)/shard_map/all_to_all | solution.py:31
  74.1 0.2 copy.44
  74.3 1.5 %fusion.5 = f32[4,128,4,32,1]{1,3,4,2,0:T(8,128)S(1)} fusion(bf16[4,8,32,128,1]{3,2,1,0,4:T(8,128)(2,1)S(1)} %bitcast.151, bf16[16,8,128,128]{3,2,1,0:T(8,128)(2,1)} %param.13, s32[]{:T(128)S(6)} %select_n.46), kind=kOutput, calls=%fused_computation.18 | convolution fusion | flops 134217728 | bytes 1572868 | tf_op jit(solution)/shard_map/ghfs,bhsd->bgfd/dot_general | solution.py:234
  75.9 0.9 middle.1
  76.8 0.3 collective-permute-start.11
  77.1 1.8 %collective-permute-start.10 = (bf16[192,128]{1,0:T(8,128)(2,1)S(1)}, bf16[192,128]{1,0:T(8,128)(2,1)S(1)}, u32[]{:S(2)}, u32[]{:S(2)}) collective-permute-start(bf16[192,128]{1,0:T(8,128)(2,1)S(1)} %get-tuple-element.37), channel_id=1, source_target_pairs={{0,2},{1,3},{2,0},{3,1},{4,6},{5,7},{6,4},{7,5},{8,10},{9,11},{10,... | collective-permute-start | bytes 147464 | tf_op jit(solution)/shard_map/ppermute | solution.py:23
  79.0 1.2 collective-permute-start.9
  80.2 0.9 collective-permute-done.11
  81.1 0.5 collective-permute-done.10
  81.6 0.9 collective-permute-done.9
  82.5 0.6 gather_fusion.3
  83.1 3.6 %fusion.2 = bf16[32,8,128]{2,0,1:T(8,128)(2,1)S(1)} fusion(bf16[16,32,128,1]{2,1,3,0:T(8,128)(2,1)S(1)} %bitcast.139, bf16[16,8,128,128]{3,2,1,0:T(8,128)(2,1)} %param.13), kind=kOutput, calls=%fused_computation.14 | convolution fusion | flops 134250496 | bytes 4390912 | tf_op jit(solution)/shard_map/bfd,bhsd->hfs/dot_general | solution.py:249
  86.8 1.5 %convolution_convert_fusion = bf16[16,32,8,128]{3,1,2,0:T(8,128)(2,1)S(1)} fusion(bf16[16,32,128,1]{2,1,3,0:T(8,128)(2,1)S(1)} %bitcast.140, bf16[16,8,128,128]{3,2,1,0:T(8,128)(2,1)S(1)} %copy-done.1), kind=kOutput, calls=%fused_computation.6 | convolution fusion | flops 134742016 | bytes 5373952 | tf_op jit(solution)/shard_map/bfd,bjsd->bjfs/dot_general | solution.py:245
  88.5 0.8 gather_fusion.4
  89.3 1.2 pad_maximum_fusion
  90.5 7.6 %all-to-all-start.2 = ((bf16[64,69,128]{2,1,0:T(8,128)(2,1)}), bf16[64,69,128]{2,1,0:T(8,128)(2,1)S(1)}, u32[]{:S(2)}, u32[]{:S(2)}) async-start(bf16[64,69,128]{2,1,0:T(8,128)(2,1)} %pad_maximum_fusion), calls=%async_computation.2 | async-start | bytes 2359296 | tf_op jit(solution)/shard_map/all_to_all | solution.py:18
  98.1 1.5 %collective-permute-start.8 = (bf16[64,512]{1,0:T(8,128)(2,1)S(1)}, bf16[64,512]{1,0:T(8,128)(2,1)S(1)}, u32[]{:S(2)}, u32[]{:S(2)}) collective-permute-start(bf16[64,512]{1,0:T(8,128)(2,1)S(1)} %get-tuple-element.28), channel_id=1, source_target_pairs={{0,3},{1,2},{2,1},{3,0},{4,7},{5,6},{6,5},{7,4},{8,11},{9,10},{10,... | collective-permute-start | bytes 196616 | tf_op jit(solution)/shard_map/ppermute | solution.py:23
  99.7 1.1 collective-permute-start.7
  100.8 0.7 collective-permute-start.6
  101.5 1.4 collective-permute-done.8
  102.8 1.4 collective-permute-done.7
  104.3 0.3 collective-permute-done.6
  104.6 0.6 gather_fusion.2
  105.2 0.7 copy.63
  105.9 23.5 %all-to-all-done.2 = bf16[64,69,128]{2,1,0:T(8,128)(2,1)S(1)} async-done(((bf16[64,69,128]{2,1,0:T(8,128)(2,1)}), bf16[64,69,128]{2,1,0:T(8,128)(2,1)S(1)}, u32[]{:S(2)}, u32[]{:S(2)}) %all-to-all-start.2) | async-done | bytes 1130528 | tf_op jit(solution)/shard_map/all_to_all | solution.py:18
  129.6 0.7 broadcast_in_dim.23
  130.2 6.2 %all-to-all-start.3 = ((bf16[64,5,128]{2,1,0:T(8,128)(2,1)}), bf16[64,5,128]{2,1,0:T(8,128)(2,1)S(1)}, u32[]{:S(2)}, u32[]{:S(2)}) async-start(bf16[64,5,128]{2,1,0:T(8,128)(2,1)} %broadcast_in_dim.23), calls=%async_computation.3 | async-start | bytes 262144 | tf_op jit(solution)/shard_map/all_to_all | solution.py:31
  136.6 0.4 fusion.7
  137.0 0.4 fusion
  137.4 9.4 %all-to-all-done.3.sums_ref = bf16[64,5,128]{2,1,0:T(8,128)(2,1)S(1)} async-done(((bf16[64,5,128]{2,1,0:T(8,128)(2,1)}), bf16[64,5,128]{2,1,0:T(8,128)(2,1)S(1)}, u32[]{:S(2)}, u32[]{:S(2)}) %all-to-all-start.3) | async-done | bytes 81952 | tf_op jit(solution)/shard_map/all_to_all | solution.py:31
  146.8 1.4 finish.1
  (64 shorter events, 1.9 us)
Async XLA Ops:
  0.6 61.5 %copy-start = (bf16[16,128,128]{2,1,0:T(8,128)(2,1)S(1)}, bf16[16,128,128]{2,1,0:T(8,128)(2,1)}, u32[]{:S(2)}) copy-start(bf16[16,128,128]{2,1,0:T(8,128)(2,1)} %param.12) | copy-start | bytes 1572868
  0.6 16.4 %copy-start.3 = (bf16[64,2048]{1,0:T(8,128)(2,1)S(1)}, bf16[64,2048]{1,0:T(8,128)(2,1)}, u32[]{:S(2)}) copy-start(bf16[64,2048]{1,0:T(8,128)(2,1)} %param.11) | copy-start | bytes 786436
  3.8 14.0 %copy-start.4 = (bf16[128,64]{0,1:T(8,128)(2,1)S(1)}, bf16[128,64]{0,1:T(8,128)(2,1)}, u32[]{:S(2)}) copy-start(bf16[128,64]{0,1:T(8,128)(2,1)} %param.10) | copy-start | bytes 49156
  3.8 18.1 %copy-start.5 = (s32[1,64,2]{1,2,0:T(2,128)S(1)}, s32[1,64,2]{1,2,0:T(2,128)}, u32[]{:S(2)}) copy-start(s32[1,64,2]{1,2,0:T(2,128)} %param.16) | copy-start | bytes 1540
  3.8 18.3 %copy-start.6 = (s32[8]{0:T(128)S(1)}, s32[8]{0:T(128)}, u32[]{:S(2)}) copy-start(s32[8]{0:T(128)} %hubs_ref.1) | copy-start | bytes 100
  3.8 44.5 %all-to-all-start = ((bf16[64,72,128]{2,1,0:T(8,128)(2,1)}), bf16[64,72,128]{2,1,0:T(8,128)(2,1)S(1)}, u32[]{:S(2)}, u32[]{:S(2)}) async-start(bf16[64,72,128]{2,1,0:T(8,128)(2,1)} %pack.1), calls=%async_computation | async-start | bytes 2359296 | tf_op jit(solution)/shard_map/all_to_all | solution.py:18
  17.9 30.8 %copy-start.7 = (s32[1,128]{1,0:T(1,128)S(1)}, s32[1,128]{1,0:T(1,128)}, u32[]{:S(2)}) copy-start(s32[1,128]{1,0:T(1,128)} %param.17) | copy-start | bytes 1540
  17.9 4.5 %collective-permute-start = (bf16[64,640]{1,0:T(8,128)(2,1)S(1)}, bf16[64,640]{1,0:T(8,128)(2,1)S(1)}, u32[]{:S(2)}, u32[]{:S(2)}) collective-permute-start(bf16[64,640]{1,0:T(8,128)(2,1)S(1)} %get-tuple-element.43), channel_id=1, source_target_pairs={{0,1},{1,0},{2,3},{3,2},{4,5},{5,4},{6,7},{7,6},{8,9},{9,8},{10,11... | collective-permute-start | bytes 245768 | tf_op jit(solution)/shard_map/ppermute | solution.py:23
  19.3 6.5 %collective-permute-start.1 = (bf16[64,640]{1,0:T(8,128)(2,1)S(1)}, bf16[64,640]{1,0:T(8,128)(2,1)S(1)}, u32[]{:S(2)}, u32[]{:S(2)}) collective-permute-start(bf16[64,640]{1,0:T(8,128)(2,1)S(1)} %get-tuple-element.44), channel_id=1, source_target_pairs={{0,2},{1,3},{2,0},{3,1},{4,6},{5,7},{6,4},{7,5},{8,10},{9,11},{10,... | collective-permute-start | bytes 245768 | tf_op jit(solution)/shard_map/ppermute | solution.py:23
  21.9 5.8 %collective-permute-start.2 = (bf16[64,640]{1,0:T(8,128)(2,1)S(1)}, bf16[64,640]{1,0:T(8,128)(2,1)S(1)}, u32[]{:S(2)}, u32[]{:S(2)}) collective-permute-start(bf16[64,640]{1,0:T(8,128)(2,1)S(1)} %get-tuple-element.45), channel_id=1, source_target_pairs={{0,3},{1,2},{2,1},{3,0},{4,7},{5,6},{6,5},{7,4},{8,11},{9,10},{10,... | collective-permute-start | bytes 245768 | tf_op jit(solution)/shard_map/ppermute | solution.py:23
  49.5 24.6 %all-to-all-start.1 = ((bf16[256,4,128]{2,1,0:T(4,128)(2,1)}), bf16[256,4,128]{2,1,0:T(4,128)(2,1)S(1)}, u32[]{:S(2)}, u32[]{:S(2)}) async-start(bf16[256,4,128]{2,1,0:T(4,128)(2,1)} %broadcast_in_dim.19), calls=%async_computation.1 | async-start | bytes 524288 | tf_op jit(solution)/shard_map/all_to_all | solution.py:31
  59.1 3.0 %copy-start.2 = (bf16[32,2048]{1,0:T(8,128)(2,1)S(1)}, bf16[32,2048]{1,0:T(8,128)(2,1)}, u32[]{:S(2)}) copy-start(bf16[32,2048]{1,0:T(8,128)(2,1)} %x_hbm.1) | copy-start | bytes 393220
  62.4 13.4 %collective-permute-start.5 = (bf16[4,32,128]{2,1,0:T(8,128)(2,1)S(1)}, bf16[4,32,128]{2,1,0:T(8,128)(2,1)S(1)}, u32[]{:S(2)}, u32[]{:S(2)}) collective-permute-start(bf16[4,32,128]{2,1,0:T(8,128)(2,1)S(1)} %get-tuple-element.39), channel_id=1, source_target_pairs={{0,3},{1,2},{2,1},{3,0},{4,7},{5,6},{6,5},{7,4},{8,11},{9,10},{10,... | collective-permute-start | bytes 98312 | tf_op jit(solution)/shard_map/ppermute | solution.py:23
  65.2 10.7 %collective-permute-start.4 = (bf16[4,32,128]{2,1,0:T(8,128)(2,1)S(1)}, bf16[4,32,128]{2,1,0:T(8,128)(2,1)S(1)}, u32[]{:S(2)}, u32[]{:S(2)}) collective-permute-start(bf16[4,32,128]{2,1,0:T(8,128)(2,1)S(1)} %get-tuple-element.40), channel_id=1, source_target_pairs={{0,2},{1,3},{2,0},{3,1},{4,6},{5,7},{6,4},{7,5},{8,10},{9,11},{10,... | collective-permute-start | bytes 98312 | tf_op jit(solution)/shard_map/ppermute | solution.py:23
  65.7 10.2 %collective-permute-start.3 = (bf16[4,32,128]{2,1,0:T(8,128)(2,1)S(1)}, bf16[4,32,128]{2,1,0:T(8,128)(2,1)S(1)}, u32[]{:S(2)}, u32[]{:S(2)}) collective-permute-start(bf16[4,32,128]{2,1,0:T(8,128)(2,1)S(1)} %get-tuple-element.41), channel_id=1, source_target_pairs={{0,1},{1,0},{2,3},{3,2},{4,5},{5,4},{6,7},{7,6},{8,9},{9,8},{10,11... | collective-permute-start | bytes 98312 | tf_op jit(solution)/shard_map/ppermute | solution.py:23
  76.8 4.2 %collective-permute-start.11 = (bf16[192,128]{1,0:T(8,128)(2,1)S(1)}, bf16[192,128]{1,0:T(8,128)(2,1)S(1)}, u32[]{:S(2)}, u32[]{:S(2)}) collective-permute-start(bf16[192,128]{1,0:T(8,128)(2,1)S(1)} %get-tuple-element.36), channel_id=1, source_target_pairs={{0,3},{1,2},{2,1},{3,0},{4,7},{5,6},{6,5},{7,4},{8,11},{9,10},{10,... | collective-permute-start | bytes 147464 | tf_op jit(solution)/shard_map/ppermute | solution.py:23
  77.1 4.4 %collective-permute-start.10 = (bf16[192,128]{1,0:T(8,128)(2,1)S(1)}, bf16[192,128]{1,0:T(8,128)(2,1)S(1)}, u32[]{:S(2)}, u32[]{:S(2)}) collective-permute-start(bf16[192,128]{1,0:T(8,128)(2,1)S(1)} %get-tuple-element.37), channel_id=1, source_target_pairs={{0,2},{1,3},{2,0},{3,1},{4,6},{5,7},{6,4},{7,5},{8,10},{9,11},{10,... | collective-permute-start | bytes 147464 | tf_op jit(solution)/shard_map/ppermute | solution.py:23
  79.0 3.5 %collective-permute-start.9 = (bf16[192,128]{1,0:T(8,128)(2,1)S(1)}, bf16[192,128]{1,0:T(8,128)(2,1)S(1)}, u32[]{:S(2)}, u32[]{:S(2)}) collective-permute-start(bf16[192,128]{1,0:T(8,128)(2,1)S(1)} %get-tuple-element.38), channel_id=1, source_target_pairs={{0,1},{1,0},{2,3},{3,2},{4,5},{5,4},{6,7},{7,6},{8,9},{9,8},{10,11... | collective-permute-start | bytes 147464 | tf_op jit(solution)/shard_map/ppermute | solution.py:23
  83.1 3.7 %copy-start.1 = (bf16[16,8,128,128]{3,2,1,0:T(8,128)(2,1)S(1)}, bf16[16,8,128,128]{3,2,1,0:T(8,128)(2,1)}, u32[]{:S(2)}) copy-start(bf16[16,8,128,128]{3,2,1,0:T(8,128)(2,1)} %param.14) | copy-start | bytes 12582916
  90.5 39.0 %all-to-all-start.2 = ((bf16[64,69,128]{2,1,0:T(8,128)(2,1)}), bf16[64,69,128]{2,1,0:T(8,128)(2,1)S(1)}, u32[]{:S(2)}, u32[]{:S(2)}) async-start(bf16[64,69,128]{2,1,0:T(8,128)(2,1)} %pad_maximum_fusion), calls=%async_computation.2 | async-start | bytes 2359296 | tf_op jit(solution)/shard_map/all_to_all | solution.py:18
  98.1 4.7 %collective-permute-start.8 = (bf16[64,512]{1,0:T(8,128)(2,1)S(1)}, bf16[64,512]{1,0:T(8,128)(2,1)S(1)}, u32[]{:S(2)}, u32[]{:S(2)}) collective-permute-start(bf16[64,512]{1,0:T(8,128)(2,1)S(1)} %get-tuple-element.28), channel_id=1, source_target_pairs={{0,3},{1,2},{2,1},{3,0},{4,7},{5,6},{6,5},{7,4},{8,11},{9,10},{10,... | collective-permute-start | bytes 196616 | tf_op jit(solution)/shard_map/ppermute | solution.py:23
  99.7 4.6 %collective-permute-start.7 = (bf16[64,512]{1,0:T(8,128)(2,1)S(1)}, bf16[64,512]{1,0:T(8,128)(2,1)S(1)}, u32[]{:S(2)}, u32[]{:S(2)}) collective-permute-start(bf16[64,512]{1,0:T(8,128)(2,1)S(1)} %get-tuple-element.29), channel_id=1, source_target_pairs={{0,2},{1,3},{2,0},{3,1},{4,6},{5,7},{6,4},{7,5},{8,10},{9,11},{10,... | collective-permute-start | bytes 196616 | tf_op jit(solution)/shard_map/ppermute | solution.py:23
  100.8 3.8 %collective-permute-start.6 = (bf16[64,512]{1,0:T(8,128)(2,1)S(1)}, bf16[64,512]{1,0:T(8,128)(2,1)S(1)}, u32[]{:S(2)}, u32[]{:S(2)}) collective-permute-start(bf16[64,512]{1,0:T(8,128)(2,1)S(1)} %get-tuple-element.30), channel_id=1, source_target_pairs={{0,1},{1,0},{2,3},{3,2},{4,5},{5,4},{6,7},{7,6},{8,9},{9,8},{10,11... | collective-permute-start | bytes 196616 | tf_op jit(solution)/shard_map/ppermute | solution.py:23
  130.2 16.6 %all-to-all-start.3 = ((bf16[64,5,128]{2,1,0:T(8,128)(2,1)}), bf16[64,5,128]{2,1,0:T(8,128)(2,1)S(1)}, u32[]{:S(2)}, u32[]{:S(2)}) async-start(bf16[64,5,128]{2,1,0:T(8,128)(2,1)} %broadcast_in_dim.23), calls=%async_computation.3 | async-start | bytes 262144 | tf_op jit(solution)/shard_map/all_to_all | solution.py:31

commit v2 on v1

--- a/solution.py
+++ b/solution.py
@@ -36,7 +36,7 @@
 VMEM = pl.BlockSpec(memory_space=pltpu.VMEM)
 
 
-def pack_kernel(sends_ref, hubs_ref, x_hbm, msg_ref, x_ref, tail_ref, sem):
+def pack_kernel(sends_ref, hubs_ref, x_hbm, out_hbm, msg_ref, x_ref, tail_ref, sem, out_sems):
     load = pltpu.make_async_copy(x_hbm, x_ref, sem)
     load.start()
     me = lax.axis_index("nodes")
@@ -58,7 +58,6 @@
 
     tail_ref[...] = jnp.zeros_like(tail_ref)
     load.wait()
-    lax.fori_loop(0, count, one, 0, unroll=8)
     for h in range(hubs):
         local = hubs_ref[h] - me * blk_count
         inside = (local >= 0) & (local < blk_count)
@@ -68,6 +67,16 @@
             place = h * (quarter // share) + i
             tail_ref[place, :share, :] = values[i * share : (i + 1) * share]
     msg_ref[:, per_dev * quarter :, :] = tail_ref[...].astype(BF)
+    lots = out_sems.shape[0]
+    size = count // lots
+    stores = []
+    for lot in range(lots):
+        lax.fori_loop(lot * size, (lot + 1) * size, one, 0, unroll=8)
+        part = pl.ds(lot * size, size)
+        stores.append(pltpu.make_async_copy(msg_ref.at[part], out_hbm.at[part], out_sems.at[lot]))
+        stores[-1].start()
+    for store in stores:
+        store.wait()
 
 
 def pack(sends, hub_ids, x_t, count, per_dev, block_len):
@@ -76,11 +85,13 @@
         pack_kernel,
         out_shape=jax.ShapeDtypeStruct((count, rows, block_len), BF),
         in_specs=[SMEM, SMEM, pl.BlockSpec(memory_space=pl.ANY)],
-        out_specs=VMEM,
+        out_specs=pl.BlockSpec(memory_space=pl.ANY),
         scratch_shapes=[
+            pltpu.VMEM((count, rows, block_len), BF),
             pltpu.VMEM(x_t.shape, x_t.dtype),
             pltpu.VMEM((count, TAIL, block_len), F32),
             pltpu.SemaphoreType.DMA,
+            pltpu.SemaphoreType.DMA((4,)),
         ],
         compiler_params=pltpu.CompilerParams(vmem_limit_bytes=56 << 20),
         name="pack",
@@ -234,10 +245,15 @@
     hub_agg = jnp.einsum("ghfs,bhsd->bgfd", hub_x, hub_share, preferred_element_type=F32)
     hub_agg = hub_agg.reshape(blk_share, feats * quarter, block_len)
     act, message = middle(row.reshape(1), hub_agg, parts, turned.reshape(feats * hid, feats * quarter), cot_share)
-    message = jnp.stack([message[0]] + [trade(message[k], k) for k in range(1, feats)])
-    upstream = message[:, : blk_share * quarter].reshape(feats, blk_share, quarter, block_len)
-    upstream = jnp.take(upstream, row ^ steps, axis=0, mode="clip")
-    upstream = upstream.reshape(blk_count, quarter, block_len)
+    messages = [message[0]] + [trade(message[k], k) for k in range(1, feats)]
+    message = jnp.stack(messages)
+    upstream = []
+    for q in range(feats):
+        share_of_q = messages[0][: blk_share * quarter]
+        for k in range(1, feats):
+            share_of_q = jnp.where(row == q ^ k, messages[k][: blk_share * quarter], share_of_q)
+        upstream.append(share_of_q)
+    upstream = jnp.concatenate(upstream, axis=0).reshape(blk_count, quarter, block_len)
     weight_sum = jnp.einsum(
         "khe,kef->hf", message[:, blk_share * quarter :], unturn, preferred_element_type=F32
     )

time: 149 us -> 148 us (level)
  matrix products: 10.9 us -> 8.71 us
  starting transfers between devices: 49.9 us -> 51.7 us
    dot_general x1, matrix products: 3.64 us -> 1.3 us  [per_device(): jnp.einsum('bfd,bhsd->hfs', upstream, hub_tiles, preferred_element_type=F32)]
  transfers between devices with their start and end apart: 16 -> 16, of which waited for: 12 -> 11; matrix products, arithmetic and copies ran while one was open for 7% -> 8% of each run, Pallas kernels for 0% -> 0%
where the time goes in v2:
time: 148 us; the launch traced here: 147 us
  waiting for transfers between devices  70.2 us (47%)
  starting transfers between devices  51.7 us (35%)
  matrix products  8.71 us (6%)
  local copies, waits for them, and re-layouts  8.57 us (6%)
  Pallas kernels  5.18 us (4%)
  other arithmetic  1.63 us (1%)
    all_to_all x2, waiting for transfers between devices, swap(): lax.all_to_all(values, 'nodes', split_axis=0, concat_axis=0, tiled=True)  43.7 us
    all_to_all x2, starting transfers between devices, swap(): lax.all_to_all(values, 'nodes', split_axis=0, concat_axis=0, tiled=True)  21.9 us
    all_to_all x2, waiting for transfers between devices, spread(): return lax.all_to_all(pieces, axes, split_axis=0, concat_axis=0, tiled=True)  16.6 us
    all_to_all x2, starting transfers between devices, spread(): return lax.all_to_all(pieces, axes, split_axis=0, concat_axis=0, tiled=True)  15 us
    ppermute x12, starting transfers between devices, trade(): return lax.ppermute(values, 'feat', [(i, i ^ step) for i in range(count)])  14.7 us
    ppermute x12, waiting for transfers between devices, trade(): return lax.ppermute(values, 'feat', [(i, i ^ step) for i in range(count)])  9.86 us
    dot_general x1, matrix products, per_device(): jnp.einsum('bjfs,bjsd->bfd', chosen, nbr_tiles, preferred_element_type=F32)  2.98 us
  transfers between devices with their start and end apart: 16, of which 11 were waited for; matrix products, arithmetic and copies ran while one was open for 8% of the time, Pallas kernels for 0%

profile of v2, /device:TPU:1, one launch (start us, length us, event | category | flops | bytes accessed | tf_op | source)
XLA Modules:
  0.0 147.2 jit_solution(14935446222255760439)
XLA Ops:
  0.7 2.9 %pack.1 = bf16[64,72,128]{2,1,0:T(8,128)(2,1)} custom-call(s32[2,64]{1,0:T(2,128)} %bitcast.180, s32[8]{0:T(128)} %hubs_ref.1, bf16[32,2048]{1,0:T(8,128)(2,1)} %x_hbm.1), custom_call_target="tpu_custom_call" | custom-call | tf_op jit(solution)/shard_map/pack/pallas_call | solution.py:84
  3.6 13.1 %all-to-all-start = ((bf16[64,72,128]{2,1,0:T(8,128)(2,1)}), bf16[64,72,128]{2,1,0:T(8,128)(2,1)S(1)}, u32[]{:S(2)}, u32[]{:S(2)}) async-start(bf16[64,72,128]{2,1,0:T(8,128)(2,1)} %pack.1), calls=%async_computation | async-start | bytes 2359296 | tf_op jit(solution)/shard_map/all_to_all | solution.py:18
  16.8 0.2 reshape.175
  17.0 0.6 constant_dynamic-slice_fusion
  17.7 1.4 collective-permute-start
  19.0 2.6 %collective-permute-start.1 = (bf16[64,640]{1,0:T(8,128)(2,1)S(1)}, bf16[64,640]{1,0:T(8,128)(2,1)S(1)}, u32[]{:S(2)}, u32[]{:S(2)}) collective-permute-start(bf16[64,640]{1,0:T(8,128)(2,1)S(1)} %get-tuple-element.47), channel_id=1, source_target_pairs={{0,2},{1,3},{2,0},{3,1},{4,6},{5,7},{6,4},{7,5},{8,10},{9,11},{10,... | collective-permute-start | bytes 245768 | tf_op jit(solution)/shard_map/ppermute | solution.py:23
  22.1 3.4 %collective-permute-done.1 = bf16[64,640]{1,0:T(8,128)(2,1)S(1)} collective-permute-done((bf16[64,640]{1,0:T(8,128)(2,1)S(1)}, bf16[64,640]{1,0:T(8,128)(2,1)S(1)}, u32[]{:S(2)}, u32[]{:S(2)}) %collective-permute-start.1) | collective-permute-done | bytes 81952 | tf_op jit(solution)/shard_map/ppermute | solution.py:23
  25.5 1.9 %collective-permute-done.2 = bf16[64,640]{1,0:T(8,128)(2,1)S(1)} collective-permute-done((bf16[64,640]{1,0:T(8,128)(2,1)S(1)}, bf16[64,640]{1,0:T(8,128)(2,1)S(1)}, u32[]{:S(2)}, u32[]{:S(2)}) %collective-permute-start.2) | collective-permute-done | bytes 81952 | tf_op jit(solution)/shard_map/ppermute | solution.py:23
  27.6 0.6 gather_fusion
  28.2 19.9 %all-to-all-done = bf16[64,72,128]{2,1,0:T(8,128)(2,1)S(1)} async-done(((bf16[64,72,128]{2,1,0:T(8,128)(2,1)}), bf16[64,72,128]{2,1,0:T(8,128)(2,1)S(1)}, u32[]{:S(2)}, u32[]{:S(2)}) %all-to-all-start) | async-done | bytes 1179680 | tf_op jit(solution)/shard_map/all_to_all | solution.py:18
  48.5 0.8 broadcast_in_dim.17
  49.3 8.9 %all-to-all-start.1 = ((bf16[256,4,128]{2,1,0:T(4,128)(2,1)}), bf16[256,4,128]{2,1,0:T(4,128)(2,1)S(1)}, u32[]{:S(2)}, u32[]{:S(2)}) async-start(bf16[256,4,128]{2,1,0:T(4,128)(2,1)} %broadcast_in_dim.17), calls=%async_computation.1 | async-start | bytes 524288 | tf_op jit(solution)/shard_map/all_to_all | solution.py:31
  58.1 0.8 gather_fusion.1
  58.9 3.0 %convolution_bitcast_fusion = f32[16,32,128]{2,1,0:T(8,128)S(1)} fusion(bf16[16,8,32,128]{3,2,1,0:T(8,128)(2,1)S(1)} %bitcast.154, bf16[16,8,128,128]{3,2,1,0:T(8,128)(2,1)} %param.14), kind=kOutput, calls=%fused_computation.10 | convolution fusion | flops 134217728 | bytes 5505024 | tf_op jit(solution)/shard_map/bjfs,bjsd->bfd/dot_general | solution.py:237
  61.9 0.3 fusion.1
  62.2 2.7 %collective-permute-start.5 = (bf16[4,32,128]{2,1,0:T(8,128)(2,1)S(1)}, bf16[4,32,128]{2,1,0:T(8,128)(2,1)S(1)}, u32[]{:S(2)}, u32[]{:S(2)}) collective-permute-start(bf16[4,32,128]{2,1,0:T(8,128)(2,1)S(1)} %get-tuple-element.42), channel_id=1, source_target_pairs={{0,3},{1,2},{2,1},{3,0},{4,7},{5,6},{6,5},{7,4},{8,11},{9,10},{10,... | collective-permute-start | bytes 98312 | tf_op jit(solution)/shard_map/ppermute | solution.py:23
  64.9 0.5 collective-permute-start.4
  65.5 0.2 collective-permute-start.3
  65.6 1.0 scatter_custom_fusion
  66.6 7.2 %all-to-all-done.1 = bf16[256,4,128]{2,1,0:T(4,128)(2,1)S(1)} async-done(((bf16[256,4,128]{2,1,0:T(4,128)(2,1)}), bf16[256,4,128]{2,1,0:T(4,128)(2,1)S(1)}, u32[]{:S(2)}, u32[]{:S(2)}) %all-to-all-start.1) | async-done | bytes 262176 | tf_op jit(solution)/shard_map/all_to_all | solution.py:31
  73.9 0.2 copy.44
  74.1 1.7 %fusion.5 = f32[4,128,4,32,1]{1,3,4,2,0:T(8,128)S(1)} fusion(bf16[4,8,32,128,1]{3,2,1,0,4:T(8,128)(2,1)S(1)} %bitcast.173, bf16[16,8,128,128]{3,2,1,0:T(8,128)(2,1)} %param.13, s32[]{:T(128)S(6)} %select_n.104), kind=kOutput, calls=%fused_computation.17 | convolution fusion | flops 134217728 | bytes 1572868 | tf_op jit(solution)/shard_map/ghfs,bhsd->bgfd/dot_general | solution.py:245
  75.8 0.9 middle.1
  76.8 0.3 collective-permute-start.11
  77.1 1.1 collective-permute-start.10
  78.3 2.4 %collective-permute-start.9 = (bf16[192,128]{1,0:T(8,128)(2,1)S(1)}, bf16[192,128]{1,0:T(8,128)(2,1)S(1)}, u32[]{:S(2)}, u32[]{:S(2)}) collective-permute-start(bf16[192,128]{1,0:T(8,128)(2,1)S(1)} %get-tuple-element.41), channel_id=1, source_target_pairs={{0,3},{1,2},{2,1},{3,0},{4,7},{5,6},{6,5},{7,4},{8,11},{9,10},{10,... | collective-permute-start | bytes 147464 | tf_op jit(solution)/shard_map/ppermute | solution.py:23
  80.7 1.0 collective-permute-done.10
  81.7 0.7 collective-permute-done.9
  82.5 1.3 fusion.2
  83.8 0.8 copy-done.1
  84.6 1.5 %convolution_convert_fusion = bf16[16,32,8,128]{3,1,2,0:T(8,128)(2,1)S(1)} fusion(bf16[16,32,128,1]{2,1,3,0:T(8,128)(2,1)S(1)} %bitcast.160, bf16[16,8,128,128]{3,2,1,0:T(8,128)(2,1)S(1)} %copy-done.1), kind=kOutput, calls=%fused_computation.5 | convolution fusion | flops 134742016 | bytes 5373952 | tf_op jit(solution)/shard_map/bfd,bjsd->bjfs/dot_general | solution.py:261
  86.2 0.2 fusion.4
  86.4 0.8 gather_fusion.3
  87.1 1.2 pad_maximum_fusion
  88.4 8.8 %all-to-all-start.2 = ((bf16[64,69,128]{2,1,0:T(8,128)(2,1)}), bf16[64,69,128]{2,1,0:T(8,128)(2,1)S(1)}, u32[]{:S(2)}, u32[]{:S(2)}) async-start(bf16[64,69,128]{2,1,0:T(8,128)(2,1)} %pad_maximum_fusion), calls=%async_computation.2 | async-start | bytes 2359296 | tf_op jit(solution)/shard_map/all_to_all | solution.py:18
  97.2 1.4 collective-permute-start.8
  98.5 2.0 %collective-permute-start.6 = (bf16[64,512]{1,0:T(8,128)(2,1)S(1)}, bf16[64,512]{1,0:T(8,128)(2,1)S(1)}, u32[]{:S(2)}, u32[]{:S(2)}) collective-permute-start(bf16[64,512]{1,0:T(8,128)(2,1)S(1)} %get-tuple-element.33), channel_id=1, source_target_pairs={{0,1},{1,0},{2,3},{3,2},{4,5},{5,4},{6,7},{7,6},{8,9},{9,8},{10,11... | collective-permute-start | bytes 196616 | tf_op jit(solution)/shard_map/ppermute | solution.py:23
  100.5 1.4 collective-permute-done.8
  101.9 1.3 collective-permute-done.7
  103.4 0.6 gather_fusion.2
  103.9 0.7 copy.63
  104.7 23.8 %all-to-all-done.2 = bf16[64,69,128]{2,1,0:T(8,128)(2,1)S(1)} async-done(((bf16[64,69,128]{2,1,0:T(8,128)(2,1)}), bf16[64,69,128]{2,1,0:T(8,128)(2,1)S(1)}, u32[]{:S(2)}, u32[]{:S(2)}) %all-to-all-start.2) | async-done | bytes 1130528 | tf_op jit(solution)/shard_map/all_to_all | solution.py:18
  128.6 0.7 broadcast_in_dim.21
  129.2 6.2 %all-to-all-start.3 = ((bf16[64,5,128]{2,1,0:T(8,128)(2,1)}), bf16[64,5,128]{2,1,0:T(8,128)(2,1)S(1)}, u32[]{:S(2)}, u32[]{:S(2)}) async-start(bf16[64,5,128]{2,1,0:T(8,128)(2,1)} %broadcast_in_dim.21), calls=%async_computation.3 | async-start | bytes 262144 | tf_op jit(solution)/shard_map/all_to_all | solution.py:31
  135.6 0.4 fusion.7
  136.0 0.4 fusion
  136.4 9.4 %all-to-all-done.3.sums_ref = bf16[64,5,128]{2,1,0:T(8,128)(2,1)S(1)} async-done(((bf16[64,5,128]{2,1,0:T(8,128)(2,1)}), bf16[64,5,128]{2,1,0:T(8,128)(2,1)S(1)}, u32[]{:S(2)}, u32[]{:S(2)}) %all-to-all-start.3) | async-done | bytes 81952 | tf_op jit(solution)/shard_map/all_to_all | solution.py:31
  145.8 1.4 finish.1
  (66 shorter events, 1.6 us)
Async XLA Ops:
  0.6 61.3 %copy-start = (bf16[16,128,128]{2,1,0:T(8,128)(2,1)S(1)}, bf16[16,128,128]{2,1,0:T(8,128)(2,1)}, u32[]{:S(2)}) copy-start(bf16[16,128,128]{2,1,0:T(8,128)(2,1)} %param.12) | copy-start | bytes 1572868
  0.6 16.1 %copy-start.4 = (bf16[64,2048]{1,0:T(8,128)(2,1)S(1)}, bf16[64,2048]{1,0:T(8,128)(2,1)}, u32[]{:S(2)}) copy-start(bf16[64,2048]{1,0:T(8,128)(2,1)} %param.11) | copy-start | bytes 786436
  3.6 14.0 %copy-start.5 = (bf16[128,64]{0,1:T(8,128)(2,1)S(1)}, bf16[128,64]{0,1:T(8,128)(2,1)}, u32[]{:S(2)}) copy-start(bf16[128,64]{0,1:T(8,128)(2,1)} %param.10) | copy-start | bytes 49156
  3.6 18.1 %copy-start.6 = (s32[1,64,2]{1,2,0:T(2,128)S(1)}, s32[1,64,2]{1,2,0:T(2,128)}, u32[]{:S(2)}) copy-start(s32[1,64,2]{1,2,0:T(2,128)} %param.16) | copy-start | bytes 1540
  3.6 18.3 %copy-start.7 = (s32[8]{0:T(128)S(1)}, s32[8]{0:T(128)}, u32[]{:S(2)}) copy-start(s32[8]{0:T(128)} %hubs_ref.1) | copy-start | bytes 100
  3.6 44.5 %all-to-all-start = ((bf16[64,72,128]{2,1,0:T(8,128)(2,1)}), bf16[64,72,128]{2,1,0:T(8,128)(2,1)S(1)}, u32[]{:S(2)}, u32[]{:S(2)}) async-start(bf16[64,72,128]{2,1,0:T(8,128)(2,1)} %pack.1), calls=%async_computation | async-start | bytes 2359296 | tf_op jit(solution)/shard_map/all_to_all | solution.py:18
  17.6 30.8 %copy-start.8 = (s32[1,128]{1,0:T(1,128)S(1)}, s32[1,128]{1,0:T(1,128)}, u32[]{:S(2)}) copy-start(s32[1,128]{1,0:T(1,128)} %param.17) | copy-start | bytes 1540
  17.7 4.5 %collective-permute-start = (bf16[64,640]{1,0:T(8,128)(2,1)S(1)}, bf16[64,640]{1,0:T(8,128)(2,1)S(1)}, u32[]{:S(2)}, u32[]{:S(2)}) collective-permute-start(bf16[64,640]{1,0:T(8,128)(2,1)S(1)} %get-tuple-element.46), channel_id=1, source_target_pairs={{0,1},{1,0},{2,3},{3,2},{4,5},{5,4},{6,7},{7,6},{8,9},{9,8},{10,11... | collective-permute-start | bytes 245768 | tf_op jit(solution)/shard_map/ppermute | solution.py:23
  19.0 6.5 %collective-permute-start.1 = (bf16[64,640]{1,0:T(8,128)(2,1)S(1)}, bf16[64,640]{1,0:T(8,128)(2,1)S(1)}, u32[]{:S(2)}, u32[]{:S(2)}) collective-permute-start(bf16[64,640]{1,0:T(8,128)(2,1)S(1)} %get-tuple-element.47), channel_id=1, source_target_pairs={{0,2},{1,3},{2,0},{3,1},{4,6},{5,7},{6,4},{7,5},{8,10},{9,11},{10,... | collective-permute-start | bytes 245768 | tf_op jit(solution)/shard_map/ppermute | solution.py:23
  21.7 5.8 %collective-permute-start.2 = (bf16[64,640]{1,0:T(8,128)(2,1)S(1)}, bf16[64,640]{1,0:T(8,128)(2,1)S(1)}, u32[]{:S(2)}, u32[]{:S(2)}) collective-permute-start(bf16[64,640]{1,0:T(8,128)(2,1)S(1)} %get-tuple-element.48), channel_id=1, source_target_pairs={{0,3},{1,2},{2,1},{3,0},{4,7},{5,6},{6,5},{7,4},{8,11},{9,10},{10,... | collective-permute-start | bytes 245768 | tf_op jit(solution)/shard_map/ppermute | solution.py:23
  49.3 24.6 %all-to-all-start.1 = ((bf16[256,4,128]{2,1,0:T(4,128)(2,1)}), bf16[256,4,128]{2,1,0:T(4,128)(2,1)S(1)}, u32[]{:S(2)}, u32[]{:S(2)}) async-start(bf16[256,4,128]{2,1,0:T(4,128)(2,1)} %broadcast_in_dim.17), calls=%async_computation.1 | async-start | bytes 524288 | tf_op jit(solution)/shard_map/all_to_all | solution.py:31
  58.9 3.0 %copy-start.3 = (bf16[32,2048]{1,0:T(8,128)(2,1)S(1)}, bf16[32,2048]{1,0:T(8,128)(2,1)}, u32[]{:S(2)}) copy-start(bf16[32,2048]{1,0:T(8,128)(2,1)} %x_hbm.1) | copy-start | bytes 393220
  62.2 13.6 %collective-permute-start.5 = (bf16[4,32,128]{2,1,0:T(8,128)(2,1)S(1)}, bf16[4,32,128]{2,1,0:T(8,128)(2,1)S(1)}, u32[]{:S(2)}, u32[]{:S(2)}) collective-permute-start(bf16[4,32,128]{2,1,0:T(8,128)(2,1)S(1)} %get-tuple-element.42), channel_id=1, source_target_pairs={{0,3},{1,2},{2,1},{3,0},{4,7},{5,6},{6,5},{7,4},{8,11},{9,10},{10,... | collective-permute-start | bytes 98312 | tf_op jit(solution)/shard_map/ppermute | solution.py:23
  64.9 10.9 %collective-permute-start.4 = (bf16[4,32,128]{2,1,0:T(8,128)(2,1)S(1)}, bf16[4,32,128]{2,1,0:T(8,128)(2,1)S(1)}, u32[]{:S(2)}, u32[]{:S(2)}) collective-permute-start(bf16[4,32,128]{2,1,0:T(8,128)(2,1)S(1)} %get-tuple-element.43), channel_id=1, source_target_pairs={{0,2},{1,3},{2,0},{3,1},{4,6},{5,7},{6,4},{7,5},{8,10},{9,11},{10,... | collective-permute-start | bytes 98312 | tf_op jit(solution)/shard_map/ppermute | solution.py:23
  65.5 10.4 %collective-permute-start.3 = (bf16[4,32,128]{2,1,0:T(8,128)(2,1)S(1)}, bf16[4,32,128]{2,1,0:T(8,128)(2,1)S(1)}, u32[]{:S(2)}, u32[]{:S(2)}) collective-permute-start(bf16[4,32,128]{2,1,0:T(8,128)(2,1)S(1)} %get-tuple-element.44), channel_id=1, source_target_pairs={{0,1},{1,0},{2,3},{3,2},{4,5},{5,4},{6,7},{7,6},{8,9},{9,8},{10,11... | collective-permute-start | bytes 98312 | tf_op jit(solution)/shard_map/ppermute | solution.py:23
  73.8 8.6 %copy-start.2 = (bf16[16,8,128,128]{3,2,1,0:T(8,128)(2,1)S(1)}, bf16[16,8,128,128]{3,2,1,0:T(8,128)(2,1)}, u32[]{:S(2)}) copy-start(bf16[16,8,128,128]{3,2,1,0:T(8,128)(2,1)} %param.13) | copy-start | bytes 12582916
  76.8 4.0 %collective-permute-start.11 = (bf16[192,128]{1,0:T(8,128)(2,1)S(1)}, bf16[192,128]{1,0:T(8,128)(2,1)S(1)}, u32[]{:S(2)}, u32[]{:S(2)}) collective-permute-start(bf16[192,128]{1,0:T(8,128)(2,1)S(1)} %get-tuple-element.39), channel_id=1, source_target_pairs={{0,1},{1,0},{2,3},{3,2},{4,5},{5,4},{6,7},{7,6},{8,9},{9,8},{10,11... | collective-permute-start | bytes 147464 | tf_op jit(solution)/shard_map/ppermute | solution.py:23
  77.1 4.6 %collective-permute-start.10 = (bf16[192,128]{1,0:T(8,128)(2,1)S(1)}, bf16[192,128]{1,0:T(8,128)(2,1)S(1)}, u32[]{:S(2)}, u32[]{:S(2)}) collective-permute-start(bf16[192,128]{1,0:T(8,128)(2,1)S(1)} %get-tuple-element.40), channel_id=1, source_target_pairs={{0,2},{1,3},{2,0},{3,1},{4,6},{5,7},{6,4},{7,5},{8,10},{9,11},{10,... | collective-permute-start | bytes 147464 | tf_op jit(solution)/shard_map/ppermute | solution.py:23
  78.3 4.2 %collective-permute-start.9 = (bf16[192,128]{1,0:T(8,128)(2,1)S(1)}, bf16[192,128]{1,0:T(8,128)(2,1)S(1)}, u32[]{:S(2)}, u32[]{:S(2)}) collective-permute-start(bf16[192,128]{1,0:T(8,128)(2,1)S(1)} %get-tuple-element.41), channel_id=1, source_target_pairs={{0,3},{1,2},{2,1},{3,0},{4,7},{5,6},{6,5},{7,4},{8,11},{9,10},{10,... | collective-permute-start | bytes 147464 | tf_op jit(solution)/shard_map/ppermute | solution.py:23
  82.4 2.2 %copy-start.1 = (bf16[16,8,128,128]{3,2,1,0:T(8,128)(2,1)S(1)}, bf16[16,8,128,128]{3,2,1,0:T(8,128)(2,1)}, u32[]{:S(2)}) copy-start(bf16[16,8,128,128]{3,2,1,0:T(8,128)(2,1)} %param.14) | copy-start | bytes 12582916
  88.4 40.1 %all-to-all-start.2 = ((bf16[64,69,128]{2,1,0:T(8,128)(2,1)}), bf16[64,69,128]{2,1,0:T(8,128)(2,1)S(1)}, u32[]{:S(2)}, u32[]{:S(2)}) async-start(bf16[64,69,128]{2,1,0:T(8,128)(2,1)} %pad_maximum_fusion), calls=%async_computation.2 | async-start | bytes 2359296 | tf_op jit(solution)/shard_map/all_to_all | solution.py:18
  97.2 4.7 %collective-permute-start.8 = (bf16[64,512]{1,0:T(8,128)(2,1)S(1)}, bf16[64,512]{1,0:T(8,128)(2,1)S(1)}, u32[]{:S(2)}, u32[]{:S(2)}) collective-permute-start(bf16[64,512]{1,0:T(8,128)(2,1)S(1)} %get-tuple-element.31), channel_id=1, source_target_pairs={{0,3},{1,2},{2,1},{3,0},{4,7},{5,6},{6,5},{7,4},{8,11},{9,10},{10,... | collective-permute-start | bytes 196616 | tf_op jit(solution)/shard_map/ppermute | solution.py:23
  98.5 4.7 %collective-permute-start.7 = (bf16[64,512]{1,0:T(8,128)(2,1)S(1)}, bf16[64,512]{1,0:T(8,128)(2,1)S(1)}, u32[]{:S(2)}, u32[]{:S(2)}) collective-permute-start(bf16[64,512]{1,0:T(8,128)(2,1)S(1)} %get-tuple-element.32), channel_id=1, source_target_pairs={{0,2},{1,3},{2,0},{3,1},{4,6},{5,7},{6,4},{7,5},{8,10},{9,11},{10,... | collective-permute-start | bytes 196616 | tf_op jit(solution)/shard_map/ppermute | solution.py:23
  98.5 4.8 %collective-permute-start.6 = (bf16[64,512]{1,0:T(8,128)(2,1)S(1)}, bf16[64,512]{1,0:T(8,128)(2,1)S(1)}, u32[]{:S(2)}, u32[]{:S(2)}) collective-permute-start(bf16[64,512]{1,0:T(8,128)(2,1)S(1)} %get-tuple-element.33), channel_id=1, source_target_pairs={{0,1},{1,0},{2,3},{3,2},{4,5},{5,4},{6,7},{7,6},{8,9},{9,8},{10,11... | collective-permute-start | bytes 196616 | tf_op jit(solution)/shard_map/ppermute | solution.py:23
  129.2 16.6 %all-to-all-start.3 = ((bf16[64,5,128]{2,1,0:T(8,128)(2,1)}), bf16[64,5,128]{2,1,0:T(8,128)(2,1)S(1)}, u32[]{:S(2)}, u32[]{:S(2)}) async-start(bf16[64,5,128]{2,1,0:T(8,128)(2,1)} %broadcast_in_dim.21), calls=%async_computation.3 | async-start | bytes 262144 | tf_op jit(solution)/shard_map/all_to_all | solution.py:31

commit v3 on v1

--- a/solution.py
+++ b/solution.py
@@ -234,10 +234,15 @@
     hub_agg = jnp.einsum("ghfs,bhsd->bgfd", hub_x, hub_share, preferred_element_type=F32)
     hub_agg = hub_agg.reshape(blk_share, feats * quarter, block_len)
     act, message = middle(row.reshape(1), hub_agg, parts, turned.reshape(feats * hid, feats * quarter), cot_share)
-    message = jnp.stack([message[0]] + [trade(message[k], k) for k in range(1, feats)])
-    upstream = message[:, : blk_share * quarter].reshape(feats, blk_share, quarter, block_len)
-    upstream = jnp.take(upstream, row ^ steps, axis=0, mode="clip")
-    upstream = upstream.reshape(blk_count, quarter, block_len)
+    messages = [message[0]] + [trade(message[k], k) for k in range(1, feats)]
+    message = jnp.stack(messages)
+    upstream = []
+    for q in range(feats):
+        share_of_q = messages[0][: blk_share * quarter]
+        for k in range(1, feats):
+            share_of_q = jnp.where(row == q ^ k, messages[k][: blk_share * quarter], share_of_q)
+        upstream.append(share_of_q)
+    upstream = jnp.concatenate(upstream, axis=0).reshape(blk_count, quarter, block_len)
     weight_sum = jnp.einsum(
         "khe,kef->hf", message[:, blk_share * quarter :], unturn, preferred_element_type=F32
     )

time: 149 us -> 148 us (level)
  matrix products: 10.9 us -> 8.71 us
  starting transfers between devices: 49.9 us -> 51.7 us
    dot_general x1, matrix products: 3.64 us -> 1.3 us  [per_device(): jnp.einsum('bfd,bhsd->hfs', upstream, hub_tiles, preferred_element_type=F32)]
  transfers between devices with their start and end apart: 16 -> 16, of which waited for: 12 -> 11; matrix products, arithmetic and copies ran while one was open for 7% -> 8% of each run, Pallas kernels for 0% -> 0%
where the time goes in v3:
time: 148 us; the launch traced here: 147 us
  waiting for transfers between devices  70.2 us (47%)
  starting transfers between devices  51.7 us (35%)
  matrix products  8.71 us (6%)
  local copies, waits for them, and re-layouts  8.57 us (6%)
  Pallas kernels  5.39 us (4%)
  other arithmetic  1.63 us (1%)
    all_to_all x2, waiting for transfers between devices, swap(): lax.all_to_all(values, 'nodes', split_axis=0, concat_axis=0, tiled=True)  43.7 us
    all_to_all x2, starting transfers between devices, swap(): lax.all_to_all(values, 'nodes', split_axis=0, concat_axis=0, tiled=True)  21.9 us
    all_to_all x2, waiting for transfers between devices, spread(): return lax.all_to_all(pieces, axes, split_axis=0, concat_axis=0, tiled=True)  16.6 us
    all_to_all x2, starting transfers between devices, spread(): return lax.all_to_all(pieces, axes, split_axis=0, concat_axis=0, tiled=True)  15 us
    ppermute x12, starting transfers between devices, trade(): return lax.ppermute(values, 'feat', [(i, i ^ step) for i in range(count)])  14.7 us
    ppermute x12, waiting for transfers between devices, trade(): return lax.ppermute(values, 'feat', [(i, i ^ step) for i in range(count)])  9.86 us
    pallas_call x1, Pallas kernels, pack(): pl.pallas_call(pack_kernel, out_shape=jax.ShapeDtypeStruct((count, rows,...  3.14 us
    dot_general x1, matrix products, per_device(): jnp.einsum('bjfs,bjsd->bfd', chosen, nbr_tiles, preferred_element_type=F32)  2.98 us
  transfers between devices with their start and end apart: 16, of which 11 were waited for; matrix products, arithmetic and copies ran while one was open for 8% of the time, Pallas kernels for 0%

profile of v3, /device:TPU:1, one launch (start us, length us, event | category | flops | bytes accessed | tf_op | source)
XLA Modules:
  0.0 147.4 jit_solution(16648219092287390565)
XLA Ops:
  0.7 3.1 %pack.1 = bf16[64,72,128]{2,1,0:T(8,128)(2,1)} custom-call(s32[2,64]{1,0:T(2,128)} %bitcast.180, s32[8]{0:T(128)} %hubs_ref.1, bf16[32,2048]{1,0:T(8,128)(2,1)} %x_hbm.1), custom_call_target="tpu_custom_call" | custom-call | tf_op jit(solution)/shard_map/pack/pallas_call | solution.py:75
  3.8 13.1 %all-to-all-start = ((bf16[64,72,128]{2,1,0:T(8,128)(2,1)}), bf16[64,72,128]{2,1,0:T(8,128)(2,1)S(1)}, u32[]{:S(2)}, u32[]{:S(2)}) async-start(bf16[64,72,128]{2,1,0:T(8,128)(2,1)} %pack.1), calls=%async_computation | async-start | bytes 2359296 | tf_op jit(solution)/shard_map/all_to_all | solution.py:18
  17.0 0.2 reshape.175
  17.2 0.6 constant_dynamic-slice_fusion
  17.9 1.4 collective-permute-start
  19.2 2.6 %collective-permute-start.1 = (bf16[64,640]{1,0:T(8,128)(2,1)S(1)}, bf16[64,640]{1,0:T(8,128)(2,1)S(1)}, u32[]{:S(2)}, u32[]{:S(2)}) collective-permute-start(bf16[64,640]{1,0:T(8,128)(2,1)S(1)} %get-tuple-element.47), channel_id=1, source_target_pairs={{0,2},{1,3},{2,0},{3,1},{4,6},{5,7},{6,4},{7,5},{8,10},{9,11},{10,... | collective-permute-start | bytes 245768 | tf_op jit(solution)/shard_map/ppermute | solution.py:23
  22.3 3.4 %collective-permute-done.1 = bf16[64,640]{1,0:T(8,128)(2,1)S(1)} collective-permute-done((bf16[64,640]{1,0:T(8,128)(2,1)S(1)}, bf16[64,640]{1,0:T(8,128)(2,1)S(1)}, u32[]{:S(2)}, u32[]{:S(2)}) %collective-permute-start.1) | collective-permute-done | bytes 81952 | tf_op jit(solution)/shard_map/ppermute | solution.py:23
  25.7 1.9 %collective-permute-done.2 = bf16[64,640]{1,0:T(8,128)(2,1)S(1)} collective-permute-done((bf16[64,640]{1,0:T(8,128)(2,1)S(1)}, bf16[64,640]{1,0:T(8,128)(2,1)S(1)}, u32[]{:S(2)}, u32[]{:S(2)}) %collective-permute-start.2) | collective-permute-done | bytes 81952 | tf_op jit(solution)/shard_map/ppermute | solution.py:23
  27.8 0.6 gather_fusion
  28.4 19.9 %all-to-all-done = bf16[64,72,128]{2,1,0:T(8,128)(2,1)S(1)} async-done(((bf16[64,72,128]{2,1,0:T(8,128)(2,1)}), bf16[64,72,128]{2,1,0:T(8,128)(2,1)S(1)}, u32[]{:S(2)}, u32[]{:S(2)}) %all-to-all-start) | async-done | bytes 1179680 | tf_op jit(solution)/shard_map/all_to_all | solution.py:18
  48.7 0.8 broadcast_in_dim.17
  49.5 8.9 %all-to-all-start.1 = ((bf16[256,4,128]{2,1,0:T(4,128)(2,1)}), bf16[256,4,128]{2,1,0:T(4,128)(2,1)S(1)}, u32[]{:S(2)}, u32[]{:S(2)}) async-start(bf16[256,4,128]{2,1,0:T(4,128)(2,1)} %broadcast_in_dim.17), calls=%async_computation.1 | async-start | bytes 524288 | tf_op jit(solution)/shard_map/all_to_all | solution.py:31
  58.3 0.8 gather_fusion.1
  59.1 3.0 %convolution_bitcast_fusion = f32[16,32,128]{2,1,0:T(8,128)S(1)} fusion(bf16[16,8,32,128]{3,2,1,0:T(8,128)(2,1)S(1)} %bitcast.154, bf16[16,8,128,128]{3,2,1,0:T(8,128)(2,1)} %param.14), kind=kOutput, calls=%fused_computation.10 | convolution fusion | flops 134217728 | bytes 5505024 | tf_op jit(solution)/shard_map/bjfs,bjsd->bfd/dot_general | solution.py:226
  62.1 0.3 fusion.1
  62.4 2.7 %collective-permute-start.5 = (bf16[4,32,128]{2,1,0:T(8,128)(2,1)S(1)}, bf16[4,32,128]{2,1,0:T(8,128)(2,1)S(1)}, u32[]{:S(2)}, u32[]{:S(2)}) collective-permute-start(bf16[4,32,128]{2,1,0:T(8,128)(2,1)S(1)} %get-tuple-element.42), channel_id=1, source_target_pairs={{0,3},{1,2},{2,1},{3,0},{4,7},{5,6},{6,5},{7,4},{8,11},{9,10},{10,... | collective-permute-start | bytes 98312 | tf_op jit(solution)/shard_map/ppermute | solution.py:23
  65.1 0.5 collective-permute-start.4
  65.7 0.2 collective-permute-start.3
  65.8 1.0 scatter_custom_fusion
  66.8 7.2 %all-to-all-done.1 = bf16[256,4,128]{2,1,0:T(4,128)(2,1)S(1)} async-done(((bf16[256,4,128]{2,1,0:T(4,128)(2,1)}), bf16[256,4,128]{2,1,0:T(4,128)(2,1)S(1)}, u32[]{:S(2)}, u32[]{:S(2)}) %all-to-all-start.1) | async-done | bytes 262176 | tf_op jit(solution)/shard_map/all_to_all | solution.py:31
  74.1 0.2 copy.44
  74.3 1.7 %fusion.5 = f32[4,128,4,32,1]{1,3,4,2,0:T(8,128)S(1)} fusion(bf16[4,8,32,128,1]{3,2,1,0,4:T(8,128)(2,1)S(1)} %bitcast.173, bf16[16,8,128,128]{3,2,1,0:T(8,128)(2,1)} %param.13, s32[]{:T(128)S(6)} %select_n.104), kind=kOutput, calls=%fused_computation.17 | convolution fusion | flops 134217728 | bytes 1572868 | tf_op jit(solution)/shard_map/ghfs,bhsd->bgfd/dot_general | solution.py:234
  76.0 0.9 middle.1
  77.0 0.3 collective-permute-start.11
  77.3 1.1 collective-permute-start.10
  78.5 2.4 %collective-permute-start.9 = (bf16[192,128]{1,0:T(8,128)(2,1)S(1)}, bf16[192,128]{1,0:T(8,128)(2,1)S(1)}, u32[]{:S(2)}, u32[]{:S(2)}) collective-permute-start(bf16[192,128]{1,0:T(8,128)(2,1)S(1)} %get-tuple-element.41), channel_id=1, source_target_pairs={{0,3},{1,2},{2,1},{3,0},{4,7},{5,6},{6,5},{7,4},{8,11},{9,10},{10,... | collective-permute-start | bytes 147464 | tf_op jit(solution)/shard_map/ppermute | solution.py:23
  80.9 1.0 collective-permute-done.10
  81.9 0.7 collective-permute-done.9
  82.7 1.3 fusion.2
  84.0 0.8 copy-done.1
  84.8 1.5 %convolution_convert_fusion = bf16[16,32,8,128]{3,1,2,0:T(8,128)(2,1)S(1)} fusion(bf16[16,32,128,1]{2,1,3,0:T(8,128)(2,1)S(1)} %bitcast.160, bf16[16,8,128,128]{3,2,1,0:T(8,128)(2,1)S(1)} %copy-done.1), kind=kOutput, calls=%fused_computation.5 | convolution fusion | flops 134742016 | bytes 5373952 | tf_op jit(solution)/shard_map/bfd,bjsd->bjfs/dot_general | solution.py:250
  86.4 0.2 fusion.4
  86.6 0.8 gather_fusion.3
  87.4 1.2 pad_maximum_fusion
  88.6 8.8 %all-to-all-start.2 = ((bf16[64,69,128]{2,1,0:T(8,128)(2,1)}), bf16[64,69,128]{2,1,0:T(8,128)(2,1)S(1)}, u32[]{:S(2)}, u32[]{:S(2)}) async-start(bf16[64,69,128]{2,1,0:T(8,128)(2,1)} %pad_maximum_fusion), calls=%async_computation.2 | async-start | bytes 2359296 | tf_op jit(solution)/shard_map/all_to_all | solution.py:18
  97.4 1.4 collective-permute-start.8
  98.7 2.0 %collective-permute-start.6 = (bf16[64,512]{1,0:T(8,128)(2,1)S(1)}, bf16[64,512]{1,0:T(8,128)(2,1)S(1)}, u32[]{:S(2)}, u32[]{:S(2)}) collective-permute-start(bf16[64,512]{1,0:T(8,128)(2,1)S(1)} %get-tuple-element.33), channel_id=1, source_target_pairs={{0,1},{1,0},{2,3},{3,2},{4,5},{5,4},{6,7},{7,6},{8,9},{9,8},{10,11... | collective-permute-start | bytes 196616 | tf_op jit(solution)/shard_map/ppermute | solution.py:23
  100.7 1.4 collective-permute-done.8
  102.1 1.3 collective-permute-done.7
  103.6 0.6 gather_fusion.2
  104.1 0.7 copy.63
  104.9 23.8 %all-to-all-done.2 = bf16[64,69,128]{2,1,0:T(8,128)(2,1)S(1)} async-done(((bf16[64,69,128]{2,1,0:T(8,128)(2,1)}), bf16[64,69,128]{2,1,0:T(8,128)(2,1)S(1)}, u32[]{:S(2)}, u32[]{:S(2)}) %all-to-all-start.2) | async-done | bytes 1130528 | tf_op jit(solution)/shard_map/all_to_all | solution.py:18
  128.8 0.7 broadcast_in_dim.21
  129.5 6.2 %all-to-all-start.3 = ((bf16[64,5,128]{2,1,0:T(8,128)(2,1)}), bf16[64,5,128]{2,1,0:T(8,128)(2,1)S(1)}, u32[]{:S(2)}, u32[]{:S(2)}) async-start(bf16[64,5,128]{2,1,0:T(8,128)(2,1)} %broadcast_in_dim.21), calls=%async_computation.3 | async-start | bytes 262144 | tf_op jit(solution)/shard_map/all_to_all | solution.py:31
  135.8 0.4 fusion.7
  136.2 0.4 fusion
  136.6 9.4 %all-to-all-done.3.sums_ref = bf16[64,5,128]{2,1,0:T(8,128)(2,1)S(1)} async-done(((bf16[64,5,128]{2,1,0:T(8,128)(2,1)}), bf16[64,5,128]{2,1,0:T(8,128)(2,1)S(1)}, u32[]{:S(2)}, u32[]{:S(2)}) %all-to-all-start.3) | async-done | bytes 81952 | tf_op jit(solution)/shard_map/all_to_all | solution.py:31
  146.0 1.4 finish.1
  (66 shorter events, 1.6 us)
Async XLA Ops:
  0.6 61.5 %copy-start = (bf16[16,128,128]{2,1,0:T(8,128)(2,1)S(1)}, bf16[16,128,128]{2,1,0:T(8,128)(2,1)}, u32[]{:S(2)}) copy-start(bf16[16,128,128]{2,1,0:T(8,128)(2,1)} %param.12) | copy-start | bytes 1572868
  0.6 16.3 %copy-start.4 = (bf16[64,2048]{1,0:T(8,128)(2,1)S(1)}, bf16[64,2048]{1,0:T(8,128)(2,1)}, u32[]{:S(2)}) copy-start(bf16[64,2048]{1,0:T(8,128)(2,1)} %param.11) | copy-start | bytes 786436
  3.8 14.0 %copy-start.5 = (bf16[128,64]{0,1:T(8,128)(2,1)S(1)}, bf16[128,64]{0,1:T(8,128)(2,1)}, u32[]{:S(2)}) copy-start(bf16[128,64]{0,1:T(8,128)(2,1)} %param.10) | copy-start | bytes 49156
  3.8 18.1 %copy-start.6 = (s32[1,64,2]{1,2,0:T(2,128)S(1)}, s32[1,64,2]{1,2,0:T(2,128)}, u32[]{:S(2)}) copy-start(s32[1,64,2]{1,2,0:T(2,128)} %param.16) | copy-start | bytes 1540
  3.8 18.3 %copy-start.7 = (s32[8]{0:T(128)S(1)}, s32[8]{0:T(128)}, u32[]{:S(2)}) copy-start(s32[8]{0:T(128)} %hubs_ref.1) | copy-start | bytes 100
  3.8 44.5 %all-to-all-start = ((bf16[64,72,128]{2,1,0:T(8,128)(2,1)}), bf16[64,72,128]{2,1,0:T(8,128)(2,1)S(1)}, u32[]{:S(2)}, u32[]{:S(2)}) async-start(bf16[64,72,128]{2,1,0:T(8,128)(2,1)} %pack.1), calls=%async_computation | async-start | bytes 2359296 | tf_op jit(solution)/shard_map/all_to_all | solution.py:18
  17.8 30.8 %copy-start.8 = (s32[1,128]{1,0:T(1,128)S(1)}, s32[1,128]{1,0:T(1,128)}, u32[]{:S(2)}) copy-start(s32[1,128]{1,0:T(1,128)} %param.17) | copy-start | bytes 1540
  17.9 4.5 %collective-permute-start = (bf16[64,640]{1,0:T(8,128)(2,1)S(1)}, bf16[64,640]{1,0:T(8,128)(2,1)S(1)}, u32[]{:S(2)}, u32[]{:S(2)}) collective-permute-start(bf16[64,640]{1,0:T(8,128)(2,1)S(1)} %get-tuple-element.46), channel_id=1, source_target_pairs={{0,1},{1,0},{2,3},{3,2},{4,5},{5,4},{6,7},{7,6},{8,9},{9,8},{10,11... | collective-permute-start | bytes 245768 | tf_op jit(solution)/shard_map/ppermute | solution.py:23
  19.2 6.5 %collective-permute-start.1 = (bf16[64,640]{1,0:T(8,128)(2,1)S(1)}, bf16[64,640]{1,0:T(8,128)(2,1)S(1)}, u32[]{:S(2)}, u32[]{:S(2)}) collective-permute-start(bf16[64,640]{1,0:T(8,128)(2,1)S(1)} %get-tuple-element.47), channel_id=1, source_target_pairs={{0,2},{1,3},{2,0},{3,1},{4,6},{5,7},{6,4},{7,5},{8,10},{9,11},{10,... | collective-permute-start | bytes 245768 | tf_op jit(solution)/shard_map/ppermute | solution.py:23
  21.9 5.8 %collective-permute-start.2 = (bf16[64,640]{1,0:T(8,128)(2,1)S(1)}, bf16[64,640]{1,0:T(8,128)(2,1)S(1)}, u32[]{:S(2)}, u32[]{:S(2)}) collective-permute-start(bf16[64,640]{1,0:T(8,128)(2,1)S(1)} %get-tuple-element.48), channel_id=1, source_target_pairs={{0,3},{1,2},{2,1},{3,0},{4,7},{5,6},{6,5},{7,4},{8,11},{9,10},{10,... | collective-permute-start | bytes 245768 | tf_op jit(solution)/shard_map/ppermute | solution.py:23
  49.5 24.6 %all-to-all-start.1 = ((bf16[256,4,128]{2,1,0:T(4,128)(2,1)}), bf16[256,4,128]{2,1,0:T(4,128)(2,1)S(1)}, u32[]{:S(2)}, u32[]{:S(2)}) async-start(bf16[256,4,128]{2,1,0:T(4,128)(2,1)} %broadcast_in_dim.17), calls=%async_computation.1 | async-start | bytes 524288 | tf_op jit(solution)/shard_map/all_to_all | solution.py:31
  59.1 3.0 %copy-start.3 = (bf16[32,2048]{1,0:T(8,128)(2,1)S(1)}, bf16[32,2048]{1,0:T(8,128)(2,1)}, u32[]{:S(2)}) copy-start(bf16[32,2048]{1,0:T(8,128)(2,1)} %x_hbm.1) | copy-start | bytes 393220
  62.4 13.6 %collective-permute-start.5 = (bf16[4,32,128]{2,1,0:T(8,128)(2,1)S(1)}, bf16[4,32,128]{2,1,0:T(8,128)(2,1)S(1)}, u32[]{:S(2)}, u32[]{:S(2)}) collective-permute-start(bf16[4,32,128]{2,1,0:T(8,128)(2,1)S(1)} %get-tuple-element.42), channel_id=1, source_target_pairs={{0,3},{1,2},{2,1},{3,0},{4,7},{5,6},{6,5},{7,4},{8,11},{9,10},{10,... | collective-permute-start | bytes 98312 | tf_op jit(solution)/shard_map/ppermute | solution.py:23
  65.1 10.9 %collective-permute-start.4 = (bf16[4,32,128]{2,1,0:T(8,128)(2,1)S(1)}, bf16[4,32,128]{2,1,0:T(8,128)(2,1)S(1)}, u32[]{:S(2)}, u32[]{:S(2)}) collective-permute-start(bf16[4,32,128]{2,1,0:T(8,128)(2,1)S(1)} %get-tuple-element.43), channel_id=1, source_target_pairs={{0,2},{1,3},{2,0},{3,1},{4,6},{5,7},{6,4},{7,5},{8,10},{9,11},{10,... | collective-permute-start | bytes 98312 | tf_op jit(solution)/shard_map/ppermute | solution.py:23
  65.7 10.4 %collective-permute-start.3 = (bf16[4,32,128]{2,1,0:T(8,128)(2,1)S(1)}, bf16[4,32,128]{2,1,0:T(8,128)(2,1)S(1)}, u32[]{:S(2)}, u32[]{:S(2)}) collective-permute-start(bf16[4,32,128]{2,1,0:T(8,128)(2,1)S(1)} %get-tuple-element.44), channel_id=1, source_target_pairs={{0,1},{1,0},{2,3},{3,2},{4,5},{5,4},{6,7},{7,6},{8,9},{9,8},{10,11... | collective-permute-start | bytes 98312 | tf_op jit(solution)/shard_map/ppermute | solution.py:23
  74.1 8.6 %copy-start.2 = (bf16[16,8,128,128]{3,2,1,0:T(8,128)(2,1)S(1)}, bf16[16,8,128,128]{3,2,1,0:T(8,128)(2,1)}, u32[]{:S(2)}) copy-start(bf16[16,8,128,128]{3,2,1,0:T(8,128)(2,1)} %param.13) | copy-start | bytes 12582916
  77.0 4.0 %collective-permute-start.11 = (bf16[192,128]{1,0:T(8,128)(2,1)S(1)}, bf16[192,128]{1,0:T(8,128)(2,1)S(1)}, u32[]{:S(2)}, u32[]{:S(2)}) collective-permute-start(bf16[192,128]{1,0:T(8,128)(2,1)S(1)} %get-tuple-element.39), channel_id=1, source_target_pairs={{0,1},{1,0},{2,3},{3,2},{4,5},{5,4},{6,7},{7,6},{8,9},{9,8},{10,11... | collective-permute-start | bytes 147464 | tf_op jit(solution)/shard_map/ppermute | solution.py:23
  77.3 4.6 %collective-permute-start.10 = (bf16[192,128]{1,0:T(8,128)(2,1)S(1)}, bf16[192,128]{1,0:T(8,128)(2,1)S(1)}, u32[]{:S(2)}, u32[]{:S(2)}) collective-permute-start(bf16[192,128]{1,0:T(8,128)(2,1)S(1)} %get-tuple-element.40), channel_id=1, source_target_pairs={{0,2},{1,3},{2,0},{3,1},{4,6},{5,7},{6,4},{7,5},{8,10},{9,11},{10,... | collective-permute-start | bytes 147464 | tf_op jit(solution)/shard_map/ppermute | solution.py:23
  78.5 4.2 %collective-permute-start.9 = (bf16[192,128]{1,0:T(8,128)(2,1)S(1)}, bf16[192,128]{1,0:T(8,128)(2,1)S(1)}, u32[]{:S(2)}, u32[]{:S(2)}) collective-permute-start(bf16[192,128]{1,0:T(8,128)(2,1)S(1)} %get-tuple-element.41), channel_id=1, source_target_pairs={{0,3},{1,2},{2,1},{3,0},{4,7},{5,6},{6,5},{7,4},{8,11},{9,10},{10,... | collective-permute-start | bytes 147464 | tf_op jit(solution)/shard_map/ppermute | solution.py:23
  82.7 2.2 %copy-start.1 = (bf16[16,8,128,128]{3,2,1,0:T(8,128)(2,1)S(1)}, bf16[16,8,128,128]{3,2,1,0:T(8,128)(2,1)}, u32[]{:S(2)}) copy-start(bf16[16,8,128,128]{3,2,1,0:T(8,128)(2,1)} %param.14) | copy-start | bytes 12582916
  88.6 40.1 %all-to-all-start.2 = ((bf16[64,69,128]{2,1,0:T(8,128)(2,1)}), bf16[64,69,128]{2,1,0:T(8,128)(2,1)S(1)}, u32[]{:S(2)}, u32[]{:S(2)}) async-start(bf16[64,69,128]{2,1,0:T(8,128)(2,1)} %pad_maximum_fusion), calls=%async_computation.2 | async-start | bytes 2359296 | tf_op jit(solution)/shard_map/all_to_all | solution.py:18
  97.4 4.7 %collective-permute-start.8 = (bf16[64,512]{1,0:T(8,128)(2,1)S(1)}, bf16[64,512]{1,0:T(8,128)(2,1)S(1)}, u32[]{:S(2)}, u32[]{:S(2)}) collective-permute-start(bf16[64,512]{1,0:T(8,128)(2,1)S(1)} %get-tuple-element.31), channel_id=1, source_target_pairs={{0,3},{1,2},{2,1},{3,0},{4,7},{5,6},{6,5},{7,4},{8,11},{9,10},{10,... | collective-permute-start | bytes 196616 | tf_op jit(solution)/shard_map/ppermute | solution.py:23
  98.7 4.7 %collective-permute-start.7 = (bf16[64,512]{1,0:T(8,128)(2,1)S(1)}, bf16[64,512]{1,0:T(8,128)(2,1)S(1)}, u32[]{:S(2)}, u32[]{:S(2)}) collective-permute-start(bf16[64,512]{1,0:T(8,128)(2,1)S(1)} %get-tuple-element.32), channel_id=1, source_target_pairs={{0,2},{1,3},{2,0},{3,1},{4,6},{5,7},{6,4},{7,5},{8,10},{9,11},{10,... | collective-permute-start | bytes 196616 | tf_op jit(solution)/shard_map/ppermute | solution.py:23
  98.7 4.8 %collective-permute-start.6 = (bf16[64,512]{1,0:T(8,128)(2,1)S(1)}, bf16[64,512]{1,0:T(8,128)(2,1)S(1)}, u32[]{:S(2)}, u32[]{:S(2)}) collective-permute-start(bf16[64,512]{1,0:T(8,128)(2,1)S(1)} %get-tuple-element.33), channel_id=1, source_target_pairs={{0,1},{1,0},{2,3},{3,2},{4,5},{5,4},{6,7},{7,6},{8,9},{9,8},{10,11... | collective-permute-start | bytes 196616 | tf_op jit(solution)/shard_map/ppermute | solution.py:23
  129.5 16.6 %all-to-all-start.3 = ((bf16[64,5,128]{2,1,0:T(8,128)(2,1)}), bf16[64,5,128]{2,1,0:T(8,128)(2,1)S(1)}, u32[]{:S(2)}, u32[]{:S(2)}) async-start(bf16[64,5,128]{2,1,0:T(8,128)(2,1)} %broadcast_in_dim.21), calls=%async_computation.3 | async-start | bytes 262144 | tf_op jit(solution)/shard_map/all_to_all | solution.py:31

commit v4 on v3

--- a/solution.py
+++ b/solution.py
@@ -58,7 +58,7 @@
 
     tail_ref[...] = jnp.zeros_like(tail_ref)
     load.wait()
-    lax.fori_loop(0, count, one, 0, unroll=8)
+    lax.fori_loop(0, count, one, 0, unroll=count)
     for h in range(hubs):
         local = hubs_ref[h] - me * blk_count
         inside = (local >= 0) & (local < blk_count)

time: 148 us -> 148 us (level)
  no operation moved by 1% of the time
where the time goes in v4:
time: 148 us; the launch traced here: 147 us
  waiting for transfers between devices  70.2 us (47%)
  starting transfers between devices  51.7 us (35%)
  matrix products  8.71 us (6%)
  local copies, waits for them, and re-layouts  8.57 us (6%)
  Pallas kernels  5.33 us (4%)
  other arithmetic  1.63 us (1%)
    all_to_all x2, waiting for transfers between devices, swap(): lax.all_to_all(values, 'nodes', split_axis=0, concat_axis=0, tiled=True)  43.7 us
    all_to_all x2, starting transfers between devices, swap(): lax.all_to_all(values, 'nodes', split_axis=0, concat_axis=0, tiled=True)  21.9 us
    all_to_all x2, waiting for transfers between devices, spread(): return lax.all_to_all(pieces, axes, split_axis=0, concat_axis=0, tiled=True)  16.6 us
    all_to_all x2, starting transfers between devices, spread(): return lax.all_to_all(pieces, axes, split_axis=0, concat_axis=0, tiled=True)  15 us
    ppermute x12, starting transfers between devices, trade(): return lax.ppermute(values, 'feat', [(i, i ^ step) for i in range(count)])  14.7 us
    ppermute x12, waiting for transfers between devices, trade(): return lax.ppermute(values, 'feat', [(i, i ^ step) for i in range(count)])  9.86 us
    pallas_call x1, Pallas kernels, pack(): pl.pallas_call(pack_kernel, out_shape=jax.ShapeDtypeStruct((count, rows,...  3.08 us
    dot_general x1, matrix products, per_device(): jnp.einsum('bjfs,bjsd->bfd', chosen, nbr_tiles, preferred_element_type=F32)  2.98 us
  transfers between devices with their start and end apart: 16, of which 11 were waited for; matrix products, arithmetic and copies ran while one was open for 8% of the time, Pallas kernels for 0%

profile of v4, /device:TPU:1, one launch (start us, length us, event | category | flops | bytes accessed | tf_op | source)
XLA Modules:
  0.0 147.3 jit_solution(666934218577586474)
XLA Ops:
  0.7 3.1 %pack.1 = bf16[64,72,128]{2,1,0:T(8,128)(2,1)} custom-call(s32[2,64]{1,0:T(2,128)} %bitcast.180, s32[8]{0:T(128)} %hubs_ref.1, bf16[32,2048]{1,0:T(8,128)(2,1)} %x_hbm.1), custom_call_target="tpu_custom_call" | custom-call | tf_op jit(solution)/shard_map/pack/pallas_call | solution.py:75
  3.8 13.1 %all-to-all-start = ((bf16[64,72,128]{2,1,0:T(8,128)(2,1)}), bf16[64,72,128]{2,1,0:T(8,128)(2,1)S(1)}, u32[]{:S(2)}, u32[]{:S(2)}) async-start(bf16[64,72,128]{2,1,0:T(8,128)(2,1)} %pack.1), calls=%async_computation | async-start | bytes 2359296 | tf_op jit(solution)/shard_map/all_to_all | solution.py:18
  16.9 0.2 reshape.175
  17.1 0.6 constant_dynamic-slice_fusion
  17.8 1.4 collective-permute-start
  19.2 2.6 %collective-permute-start.1 = (bf16[64,640]{1,0:T(8,128)(2,1)S(1)}, bf16[64,640]{1,0:T(8,128)(2,1)S(1)}, u32[]{:S(2)}, u32[]{:S(2)}) collective-permute-start(bf16[64,640]{1,0:T(8,128)(2,1)S(1)} %get-tuple-element.47), channel_id=1, source_target_pairs={{0,2},{1,3},{2,0},{3,1},{4,6},{5,7},{6,4},{7,5},{8,10},{9,11},{10,... | collective-permute-start | bytes 245768 | tf_op jit(solution)/shard_map/ppermute | solution.py:23
  22.3 3.4 %collective-permute-done.1 = bf16[64,640]{1,0:T(8,128)(2,1)S(1)} collective-permute-done((bf16[64,640]{1,0:T(8,128)(2,1)S(1)}, bf16[64,640]{1,0:T(8,128)(2,1)S(1)}, u32[]{:S(2)}, u32[]{:S(2)}) %collective-permute-start.1) | collective-permute-done | bytes 81952 | tf_op jit(solution)/shard_map/ppermute | solution.py:23
  25.7 1.9 %collective-permute-done.2 = bf16[64,640]{1,0:T(8,128)(2,1)S(1)} collective-permute-done((bf16[64,640]{1,0:T(8,128)(2,1)S(1)}, bf16[64,640]{1,0:T(8,128)(2,1)S(1)}, u32[]{:S(2)}, u32[]{:S(2)}) %collective-permute-start.2) | collective-permute-done | bytes 81952 | tf_op jit(solution)/shard_map/ppermute | solution.py:23
  27.7 0.6 gather_fusion
  28.4 19.9 %all-to-all-done = bf16[64,72,128]{2,1,0:T(8,128)(2,1)S(1)} async-done(((bf16[64,72,128]{2,1,0:T(8,128)(2,1)}), bf16[64,72,128]{2,1,0:T(8,128)(2,1)S(1)}, u32[]{:S(2)}, u32[]{:S(2)}) %all-to-all-start) | async-done | bytes 1179680 | tf_op jit(solution)/shard_map/all_to_all | solution.py:18
  48.6 0.8 broadcast_in_dim.17
  49.4 8.9 %all-to-all-start.1 = ((bf16[256,4,128]{2,1,0:T(4,128)(2,1)}), bf16[256,4,128]{2,1,0:T(4,128)(2,1)S(1)}, u32[]{:S(2)}, u32[]{:S(2)}) async-start(bf16[256,4,128]{2,1,0:T(4,128)(2,1)} %broadcast_in_dim.17), calls=%async_computation.1 | async-start | bytes 524288 | tf_op jit(solution)/shard_map/all_to_all | solution.py:31
  58.3 0.8 gather_fusion.1
  59.1 3.0 %convolution_bitcast_fusion = f32[16,32,128]{2,1,0:T(8,128)S(1)} fusion(bf16[16,8,32,128]{3,2,1,0:T(8,128)(2,1)S(1)} %bitcast.154, bf16[16,8,128,128]{3,2,1,0:T(8,128)(2,1)} %param.14), kind=kOutput, calls=%fused_computation.10 | convolution fusion | flops 134217728 | bytes 5505024 | tf_op jit(solution)/shard_map/bjfs,bjsd->bfd/dot_general | solution.py:226
  62.1 0.3 fusion.1
  62.4 2.7 %collective-permute-start.5 = (bf16[4,32,128]{2,1,0:T(8,128)(2,1)S(1)}, bf16[4,32,128]{2,1,0:T(8,128)(2,1)S(1)}, u32[]{:S(2)}, u32[]{:S(2)}) collective-permute-start(bf16[4,32,128]{2,1,0:T(8,128)(2,1)S(1)} %get-tuple-element.42), channel_id=1, source_target_pairs={{0,3},{1,2},{2,1},{3,0},{4,7},{5,6},{6,5},{7,4},{8,11},{9,10},{10,... | collective-permute-start | bytes 98312 | tf_op jit(solution)/shard_map/ppermute | solution.py:23
  65.1 0.5 collective-permute-start.4
  65.6 0.2 collective-permute-start.3
  65.8 1.0 scatter_custom_fusion
  66.8 7.2 %all-to-all-done.1 = bf16[256,4,128]{2,1,0:T(4,128)(2,1)S(1)} async-done(((bf16[256,4,128]{2,1,0:T(4,128)(2,1)}), bf16[256,4,128]{2,1,0:T(4,128)(2,1)S(1)}, u32[]{:S(2)}, u32[]{:S(2)}) %all-to-all-start.1) | async-done | bytes 262176 | tf_op jit(solution)/shard_map/all_to_all | solution.py:31
  74.0 0.2 copy.44
  74.2 1.7 %fusion.5 = f32[4,128,4,32,1]{1,3,4,2,0:T(8,128)S(1)} fusion(bf16[4,8,32,128,1]{3,2,1,0,4:T(8,128)(2,1)S(1)} %bitcast.173, bf16[16,8,128,128]{3,2,1,0:T(8,128)(2,1)} %param.13, s32[]{:T(128)S(6)} %select_n.104), kind=kOutput, calls=%fused_computation.17 | convolution fusion | flops 134217728 | bytes 1572868 | tf_op jit(solution)/shard_map/ghfs,bhsd->bgfd/dot_general | solution.py:234
  76.0 0.9 middle.1
  76.9 0.3 collective-permute-start.11
  77.3 1.1 collective-permute-start.10
  78.4 2.4 %collective-permute-start.9 = (bf16[192,128]{1,0:T(8,128)(2,1)S(1)}, bf16[192,128]{1,0:T(8,128)(2,1)S(1)}, u32[]{:S(2)}, u32[]{:S(2)}) collective-permute-start(bf16[192,128]{1,0:T(8,128)(2,1)S(1)} %get-tuple-element.41), channel_id=1, source_target_pairs={{0,3},{1,2},{2,1},{3,0},{4,7},{5,6},{6,5},{7,4},{8,11},{9,10},{10,... | collective-permute-start | bytes 147464 | tf_op jit(solution)/shard_map/ppermute | solution.py:23
  80.9 1.0 collective-permute-done.10
  81.8 0.7 collective-permute-done.9
  82.6 1.3 fusion.2
  83.9 0.8 copy-done.1
  84.8 1.5 %convolution_convert_fusion = bf16[16,32,8,128]{3,1,2,0:T(8,128)(2,1)S(1)} fusion(bf16[16,32,128,1]{2,1,3,0:T(8,128)(2,1)S(1)} %bitcast.160, bf16[16,8,128,128]{3,2,1,0:T(8,128)(2,1)S(1)} %copy-done.1), kind=kOutput, calls=%fused_computation.5 | convolution fusion | flops 134742016 | bytes 5373952 | tf_op jit(solution)/shard_map/bfd,bjsd->bjfs/dot_general | solution.py:250
  86.3 0.2 fusion.4
  86.5 0.8 gather_fusion.3
  87.3 1.2 pad_maximum_fusion
  88.5 8.8 %all-to-all-start.2 = ((bf16[64,69,128]{2,1,0:T(8,128)(2,1)}), bf16[64,69,128]{2,1,0:T(8,128)(2,1)S(1)}, u32[]{:S(2)}, u32[]{:S(2)}) async-start(bf16[64,69,128]{2,1,0:T(8,128)(2,1)} %pad_maximum_fusion), calls=%async_computation.2 | async-start | bytes 2359296 | tf_op jit(solution)/shard_map/all_to_all | solution.py:18
  97.3 1.4 collective-permute-start.8
  98.7 2.0 %collective-permute-start.6 = (bf16[64,512]{1,0:T(8,128)(2,1)S(1)}, bf16[64,512]{1,0:T(8,128)(2,1)S(1)}, u32[]{:S(2)}, u32[]{:S(2)}) collective-permute-start(bf16[64,512]{1,0:T(8,128)(2,1)S(1)} %get-tuple-element.33), channel_id=1, source_target_pairs={{0,1},{1,0},{2,3},{3,2},{4,5},{5,4},{6,7},{7,6},{8,9},{9,8},{10,11... | collective-permute-start | bytes 196616 | tf_op jit(solution)/shard_map/ppermute | solution.py:23
  100.6 1.4 collective-permute-done.8
  102.0 1.3 collective-permute-done.7
  103.5 0.6 gather_fusion.2
  104.1 0.7 copy.63
  104.8 23.8 %all-to-all-done.2 = bf16[64,69,128]{2,1,0:T(8,128)(2,1)S(1)} async-done(((bf16[64,69,128]{2,1,0:T(8,128)(2,1)}), bf16[64,69,128]{2,1,0:T(8,128)(2,1)S(1)}, u32[]{:S(2)}, u32[]{:S(2)}) %all-to-all-start.2) | async-done | bytes 1130528 | tf_op jit(solution)/shard_map/all_to_all | solution.py:18
  128.7 0.7 broadcast_in_dim.21
  129.4 6.2 %all-to-all-start.3 = ((bf16[64,5,128]{2,1,0:T(8,128)(2,1)}), bf16[64,5,128]{2,1,0:T(8,128)(2,1)S(1)}, u32[]{:S(2)}, u32[]{:S(2)}) async-start(bf16[64,5,128]{2,1,0:T(8,128)(2,1)} %broadcast_in_dim.21), calls=%async_computation.3 | async-start | bytes 262144 | tf_op jit(solution)/shard_map/all_to_all | solution.py:31
  135.7 0.4 fusion.7
  136.1 0.4 fusion
  136.5 9.4 %all-to-all-done.3.sums_ref = bf16[64,5,128]{2,1,0:T(8,128)(2,1)S(1)} async-done(((bf16[64,5,128]{2,1,0:T(8,128)(2,1)}), bf16[64,5,128]{2,1,0:T(8,128)(2,1)S(1)}, u32[]{:S(2)}, u32[]{:S(2)}) %all-to-all-start.3) | async-done | bytes 81952 | tf_op jit(solution)/shard_map/all_to_all | solution.py:31
  146.0 1.4 finish.1
  (66 shorter events, 1.6 us)
Async XLA Ops:
  0.6 61.4 %copy-start = (bf16[16,128,128]{2,1,0:T(8,128)(2,1)S(1)}, bf16[16,128,128]{2,1,0:T(8,128)(2,1)}, u32[]{:S(2)}) copy-start(bf16[16,128,128]{2,1,0:T(8,128)(2,1)} %param.12) | copy-start | bytes 1572868
  0.6 16.3 %copy-start.4 = (bf16[64,2048]{1,0:T(8,128)(2,1)S(1)}, bf16[64,2048]{1,0:T(8,128)(2,1)}, u32[]{:S(2)}) copy-start(bf16[64,2048]{1,0:T(8,128)(2,1)} %param.11) | copy-start | bytes 786436
  3.7 14.0 %copy-start.5 = (bf16[128,64]{0,1:T(8,128)(2,1)S(1)}, bf16[128,64]{0,1:T(8,128)(2,1)}, u32[]{:S(2)}) copy-start(bf16[128,64]{0,1:T(8,128)(2,1)} %param.10) | copy-start | bytes 49156
  3.8 18.1 %copy-start.6 = (s32[1,64,2]{1,2,0:T(2,128)S(1)}, s32[1,64,2]{1,2,0:T(2,128)}, u32[]{:S(2)}) copy-start(s32[1,64,2]{1,2,0:T(2,128)} %param.16) | copy-start | bytes 1540
  3.8 18.3 %copy-start.7 = (s32[8]{0:T(128)S(1)}, s32[8]{0:T(128)}, u32[]{:S(2)}) copy-start(s32[8]{0:T(128)} %hubs_ref.1) | copy-start | bytes 100
  3.8 44.5 %all-to-all-start = ((bf16[64,72,128]{2,1,0:T(8,128)(2,1)}), bf16[64,72,128]{2,1,0:T(8,128)(2,1)S(1)}, u32[]{:S(2)}, u32[]{:S(2)}) async-start(bf16[64,72,128]{2,1,0:T(8,128)(2,1)} %pack.1), calls=%async_computation | async-start | bytes 2359296 | tf_op jit(solution)/shard_map/all_to_all | solution.py:18
  17.8 30.8 %copy-start.8 = (s32[1,128]{1,0:T(1,128)S(1)}, s32[1,128]{1,0:T(1,128)}, u32[]{:S(2)}) copy-start(s32[1,128]{1,0:T(1,128)} %param.17) | copy-start | bytes 1540
  17.8 4.5 %collective-permute-start = (bf16[64,640]{1,0:T(8,128)(2,1)S(1)}, bf16[64,640]{1,0:T(8,128)(2,1)S(1)}, u32[]{:S(2)}, u32[]{:S(2)}) collective-permute-start(bf16[64,640]{1,0:T(8,128)(2,1)S(1)} %get-tuple-element.46), channel_id=1, source_target_pairs={{0,1},{1,0},{2,3},{3,2},{4,5},{5,4},{6,7},{7,6},{8,9},{9,8},{10,11... | collective-permute-start | bytes 245768 | tf_op jit(solution)/shard_map/ppermute | solution.py:23
  19.2 6.5 %collective-permute-start.1 = (bf16[64,640]{1,0:T(8,128)(2,1)S(1)}, bf16[64,640]{1,0:T(8,128)(2,1)S(1)}, u32[]{:S(2)}, u32[]{:S(2)}) collective-permute-start(bf16[64,640]{1,0:T(8,128)(2,1)S(1)} %get-tuple-element.47), channel_id=1, source_target_pairs={{0,2},{1,3},{2,0},{3,1},{4,6},{5,7},{6,4},{7,5},{8,10},{9,11},{10,... | collective-permute-start | bytes 245768 | tf_op jit(solution)/shard_map/ppermute | solution.py:23
  21.8 5.8 %collective-permute-start.2 = (bf16[64,640]{1,0:T(8,128)(2,1)S(1)}, bf16[64,640]{1,0:T(8,128)(2,1)S(1)}, u32[]{:S(2)}, u32[]{:S(2)}) collective-permute-start(bf16[64,640]{1,0:T(8,128)(2,1)S(1)} %get-tuple-element.48), channel_id=1, source_target_pairs={{0,3},{1,2},{2,1},{3,0},{4,7},{5,6},{6,5},{7,4},{8,11},{9,10},{10,... | collective-permute-start | bytes 245768 | tf_op jit(solution)/shard_map/ppermute | solution.py:23
  49.4 24.6 %all-to-all-start.1 = ((bf16[256,4,128]{2,1,0:T(4,128)(2,1)}), bf16[256,4,128]{2,1,0:T(4,128)(2,1)S(1)}, u32[]{:S(2)}, u32[]{:S(2)}) async-start(bf16[256,4,128]{2,1,0:T(4,128)(2,1)} %broadcast_in_dim.17), calls=%async_computation.1 | async-start | bytes 524288 | tf_op jit(solution)/shard_map/all_to_all | solution.py:31
  59.1 3.0 %copy-start.3 = (bf16[32,2048]{1,0:T(8,128)(2,1)S(1)}, bf16[32,2048]{1,0:T(8,128)(2,1)}, u32[]{:S(2)}) copy-start(bf16[32,2048]{1,0:T(8,128)(2,1)} %x_hbm.1) | copy-start | bytes 393220
  62.4 13.6 %collective-permute-start.5 = (bf16[4,32,128]{2,1,0:T(8,128)(2,1)S(1)}, bf16[4,32,128]{2,1,0:T(8,128)(2,1)S(1)}, u32[]{:S(2)}, u32[]{:S(2)}) collective-permute-start(bf16[4,32,128]{2,1,0:T(8,128)(2,1)S(1)} %get-tuple-element.42), channel_id=1, source_target_pairs={{0,3},{1,2},{2,1},{3,0},{4,7},{5,6},{6,5},{7,4},{8,11},{9,10},{10,... | collective-permute-start | bytes 98312 | tf_op jit(solution)/shard_map/ppermute | solution.py:23
  65.1 10.9 %collective-permute-start.4 = (bf16[4,32,128]{2,1,0:T(8,128)(2,1)S(1)}, bf16[4,32,128]{2,1,0:T(8,128)(2,1)S(1)}, u32[]{:S(2)}, u32[]{:S(2)}) collective-permute-start(bf16[4,32,128]{2,1,0:T(8,128)(2,1)S(1)} %get-tuple-element.43), channel_id=1, source_target_pairs={{0,2},{1,3},{2,0},{3,1},{4,6},{5,7},{6,4},{7,5},{8,10},{9,11},{10,... | collective-permute-start | bytes 98312 | tf_op jit(solution)/shard_map/ppermute | solution.py:23
  65.6 10.4 %collective-permute-start.3 = (bf16[4,32,128]{2,1,0:T(8,128)(2,1)S(1)}, bf16[4,32,128]{2,1,0:T(8,128)(2,1)S(1)}, u32[]{:S(2)}, u32[]{:S(2)}) collective-permute-start(bf16[4,32,128]{2,1,0:T(8,128)(2,1)S(1)} %get-tuple-element.44), channel_id=1, source_target_pairs={{0,1},{1,0},{2,3},{3,2},{4,5},{5,4},{6,7},{7,6},{8,9},{9,8},{10,11... | collective-permute-start | bytes 98312 | tf_op jit(solution)/shard_map/ppermute | solution.py:23
  74.0 8.6 %copy-start.2 = (bf16[16,8,128,128]{3,2,1,0:T(8,128)(2,1)S(1)}, bf16[16,8,128,128]{3,2,1,0:T(8,128)(2,1)}, u32[]{:S(2)}) copy-start(bf16[16,8,128,128]{3,2,1,0:T(8,128)(2,1)} %param.13) | copy-start | bytes 12582916
  76.9 4.0 %collective-permute-start.11 = (bf16[192,128]{1,0:T(8,128)(2,1)S(1)}, bf16[192,128]{1,0:T(8,128)(2,1)S(1)}, u32[]{:S(2)}, u32[]{:S(2)}) collective-permute-start(bf16[192,128]{1,0:T(8,128)(2,1)S(1)} %get-tuple-element.39), channel_id=1, source_target_pairs={{0,1},{1,0},{2,3},{3,2},{4,5},{5,4},{6,7},{7,6},{8,9},{9,8},{10,11... | collective-permute-start | bytes 147464 | tf_op jit(solution)/shard_map/ppermute | solution.py:23
  77.3 4.6 %collective-permute-start.10 = (bf16[192,128]{1,0:T(8,128)(2,1)S(1)}, bf16[192,128]{1,0:T(8,128)(2,1)S(1)}, u32[]{:S(2)}, u32[]{:S(2)}) collective-permute-start(bf16[192,128]{1,0:T(8,128)(2,1)S(1)} %get-tuple-element.40), channel_id=1, source_target_pairs={{0,2},{1,3},{2,0},{3,1},{4,6},{5,7},{6,4},{7,5},{8,10},{9,11},{10,... | collective-permute-start | bytes 147464 | tf_op jit(solution)/shard_map/ppermute | solution.py:23
  78.4 4.2 %collective-permute-start.9 = (bf16[192,128]{1,0:T(8,128)(2,1)S(1)}, bf16[192,128]{1,0:T(8,128)(2,1)S(1)}, u32[]{:S(2)}, u32[]{:S(2)}) collective-permute-start(bf16[192,128]{1,0:T(8,128)(2,1)S(1)} %get-tuple-element.41), channel_id=1, source_target_pairs={{0,3},{1,2},{2,1},{3,0},{4,7},{5,6},{6,5},{7,4},{8,11},{9,10},{10,... | collective-permute-start | bytes 147464 | tf_op jit(solution)/shard_map/ppermute | solution.py:23
  82.6 2.2 %copy-start.1 = (bf16[16,8,128,128]{3,2,1,0:T(8,128)(2,1)S(1)}, bf16[16,8,128,128]{3,2,1,0:T(8,128)(2,1)}, u32[]{:S(2)}) copy-start(bf16[16,8,128,128]{3,2,1,0:T(8,128)(2,1)} %param.14) | copy-start | bytes 12582916
  88.5 40.1 %all-to-all-start.2 = ((bf16[64,69,128]{2,1,0:T(8,128)(2,1)}), bf16[64,69,128]{2,1,0:T(8,128)(2,1)S(1)}, u32[]{:S(2)}, u32[]{:S(2)}) async-start(bf16[64,69,128]{2,1,0:T(8,128)(2,1)} %pad_maximum_fusion), calls=%async_computation.2 | async-start | bytes 2359296 | tf_op jit(solution)/shard_map/all_to_all | solution.py:18
  97.3 4.7 %collective-permute-start.8 = (bf16[64,512]{1,0:T(8,128)(2,1)S(1)}, bf16[64,512]{1,0:T(8,128)(2,1)S(1)}, u32[]{:S(2)}, u32[]{:S(2)}) collective-permute-start(bf16[64,512]{1,0:T(8,128)(2,1)S(1)} %get-tuple-element.31), channel_id=1, source_target_pairs={{0,3},{1,2},{2,1},{3,0},{4,7},{5,6},{6,5},{7,4},{8,11},{9,10},{10,... | collective-permute-start | bytes 196616 | tf_op jit(solution)/shard_map/ppermute | solution.py:23
  98.7 4.7 %collective-permute-start.7 = (bf16[64,512]{1,0:T(8,128)(2,1)S(1)}, bf16[64,512]{1,0:T(8,128)(2,1)S(1)}, u32[]{:S(2)}, u32[]{:S(2)}) collective-permute-start(bf16[64,512]{1,0:T(8,128)(2,1)S(1)} %get-tuple-element.32), channel_id=1, source_target_pairs={{0,2},{1,3},{2,0},{3,1},{4,6},{5,7},{6,4},{7,5},{8,10},{9,11},{10,... | collective-permute-start | bytes 196616 | tf_op jit(solution)/shard_map/ppermute | solution.py:23
  98.7 4.8 %collective-permute-start.6 = (bf16[64,512]{1,0:T(8,128)(2,1)S(1)}, bf16[64,512]{1,0:T(8,128)(2,1)S(1)}, u32[]{:S(2)}, u32[]{:S(2)}) collective-permute-start(bf16[64,512]{1,0:T(8,128)(2,1)S(1)} %get-tuple-element.33), channel_id=1, source_target_pairs={{0,1},{1,0},{2,3},{3,2},{4,5},{5,4},{6,7},{7,6},{8,9},{9,8},{10,11... | collective-permute-start | bytes 196616 | tf_op jit(solution)/shard_map/ppermute | solution.py:23
  129.4 16.6 %all-to-all-start.3 = ((bf16[64,5,128]{2,1,0:T(8,128)(2,1)}), bf16[64,5,128]{2,1,0:T(8,128)(2,1)S(1)}, u32[]{:S(2)}, u32[]{:S(2)}) async-start(bf16[64,5,128]{2,1,0:T(8,128)(2,1)} %broadcast_in_dim.21), calls=%async_computation.3 | async-start | bytes 262144 | tf_op jit(solution)/shard_map/all_to_all | solution.py:31
